TPU v7x, 128 devices: a whole 4x4x4 slice. The times are simulated.
128 devices in a mesh: slab: 16 (over z, y), pencil: 8 (over x, core).
Axes of the slice: x: 4, y: 4, z: 4, core: 2. Of those that a mesh axis runs over, the one named last changes fastest.
Arguments:
- fine_density: float32 [16, 8, 8, 64, 64, 64], P('slab', 'pencil'), may hold values from 0.1 to 10
- coarse_density: float32 [1536, 512, 128], P('slab', 'pencil'), may hold values from 0.1 to 10
- patch_anchor: int32 [16, 8, 8, 3], P('slab', 'pencil'), may hold values from 0 to 96, as said below
- patch_extent: int32 [16, 8, 8, 3], P('slab', 'pencil'), may hold values from 16 to 64, as said below
- patch_owner: int32 [16, 8, 8, 1], P('slab', 'pencil'), may hold values from 0 to 15; in each aligned block of 8 rows (0 to 7, 8 to 15, ..., all dimensions but the last counted through in order) no two rows name the same one
- patch_count: int32 [16, 8], P('slab', 'pencil'), may hold values from 6 to 8, as said below
Outputs:
- potential: float32 [1536, 512, 128], P('slab', 'pencil')
- gradient: float32 [3, 1536, 512, 128], P(None, 'slab', 'pencil')
Inputs may be any that keep to these rules, and one draw needn't show every extreme that they name: `patch_anchor`: component 0 lies in 0 to 64, component 1 in 0 to 32, component 2 in 0 to 96. `patch_extent`: even numbers. `patch_owner`: within the 8 slots of one device no two name the same slab. `patch_count`: some device has all 8 slots live.
All inputs are finite; a program needn't handle non-finite values.
Results may differ from a plain program's by a relative error of at most 0.0001.
Values sent between devices are 32-bit elements; how exact they have to be, the bound alone decides.
No kernel may reach another device: no remote copies, remote signals or barrier semaphores. Data moves between devices by JAX's collectives and lax.ppermute only.
A program may use at most 384 MiB of HBM per device.

v0:
```python
import functools

import jax
import jax.numpy as jnp
from jax import lax
from jax.experimental import pallas as pl
from jax.experimental.pallas import tpu as pltpu
from jax.sharding import PartitionSpec as P

HALO = 4
META_ROWS = 8
STEP = 8
F32 = jnp.float32


def average_kernel(meta, fine, sent, packed, blank, sems, blank_sem):
    slots = pl.num_programs(0)
    p = pl.program_id(0)
    buffer = lax.rem(p, 2)
    rows = packed.shape[1] - META_ROWS
    edge = fine.shape[3] // 2
    lanes = packed.shape[2]
    groups = lanes // edge
    tiles = edge // groups
    width = fine.shape[5]

    def blank_copy():
        return pltpu.make_async_copy(blank, sent.at[:, pl.ds(rows, META_ROWS), :], blank_sem)

    def slot_copy(patch, which):
        owner = meta[6 * slots + patch]
        return pltpu.make_async_copy(packed.at[which], sent.at[owner], sems.at[which])

    @pl.when(p == 0)
    def _():
        blank[...] = jnp.zeros_like(blank)
        blank_copy().start()

    @pl.when(p >= 2)
    def _():
        slot_copy(p - 2, buffer).wait()

    total = jnp.zeros((rows, lanes), F32)
    for g in range(groups):
        part = None
        for dx in range(2):
            for dy in range(2):
                piece = fine[0, 0, 0, pl.ds(2 * g + dx, tiles, stride=2 * groups), pl.ds(dy, edge, stride=2), :]
                part = piece if part is None else part + piece
        part = part.reshape(rows, width)
        high = part.astype(jnp.bfloat16)
        low = (part - high.astype(F32)).astype(jnp.bfloat16)
        source_lane = lax.broadcasted_iota(jnp.int32, (width, lanes), 0)
        target_lane = lax.broadcasted_iota(jnp.int32, (width, lanes), 1)
        gather = jnp.where(target_lane == g * edge + source_lane // 2, 0.125, 0.0).astype(jnp.bfloat16)
        total = total + jnp.dot(high, gather, preferred_element_type=F32)
        total = total + jnp.dot(low, gather, preferred_element_type=F32)
    packed[buffer, :rows, :] = total
    lane = lax.broadcasted_iota(jnp.int32, (META_ROWS, lanes), 1)
    alive = (p < meta[7 * slots]).astype(jnp.int32)
    words = jnp.where(lane == 0, alive, 0)
    for d in range(3):
        words = jnp.where(lane == 1 + d, meta[3 * p + d], words)
        words = jnp.where(lane == 4 + d, lax.shift_right_logical(meta[3 * (slots + p) + d], 1), words)
    packed[buffer, pl.ds(rows, META_ROWS), :] = words.astype(F32)

    @pl.when(p == 0)
    def _():
        blank_copy().wait()

    slot_copy(p, buffer).start()

    @pl.when(p == slots - 1)
    def _():
        slot_copy(p - 1, 1 - buffer).wait()
        slot_copy(p, buffer).wait()


def average(fine, meta, slabs):
    slots, fine_edge = fine.shape[2], fine.shape[3]
    edge = fine_edge // 2
    rows = edge * edge * edge // 128
    block = (1, 1, 1) + fine.shape[3:]
    return pl.pallas_call(
        average_kernel,
        out_shape=jax.ShapeDtypeStruct((slabs, rows + META_ROWS, 128), F32),
        grid_spec=pltpu.PrefetchScalarGridSpec(
            num_scalar_prefetch=1,
            grid=(slots,),
            in_specs=[pl.BlockSpec(block, lambda p, meta: (0, 0, p, 0, 0, 0))],
            out_specs=pl.BlockSpec(memory_space=pl.ANY),
            scratch_shapes=[
                pltpu.VMEM((2, rows + META_ROWS, 128), F32),
                pltpu.VMEM((slabs, META_ROWS, 128), F32),
                pltpu.SemaphoreType.DMA((2,)),
                pltpu.SemaphoreType.DMA,
            ],
        ),
        compiler_params=pltpu.CompilerParams(
            dimension_semantics=("arbitrary",), vmem_limit_bytes=32 << 20
        ),
        name="average",
    )(meta, fine)


def deposit_kernel(received, coarse, source, y_low, y_high, words, sem):
    slabs, all_rows, lanes = received.shape
    rows = all_rows - META_ROWS
    edge = 32
    groups = lanes // edge
    planes, height, _ = source.shape
    for s in range(slabs):
        pltpu.make_async_copy(received.at[s, rows], words.at[s], sem).start()
    source[...] = jnp.zeros_like(source)
    for s in range(slabs):
        pltpu.make_async_copy(received.at[s, rows], words.at[s], sem).wait()
    row = lax.broadcasted_iota(jnp.int32, (edge, lanes), 0)
    lane = lax.broadcasted_iota(jnp.int32, (edge, lanes), 1)

    @pl.loop(0, slabs)
    def _(s):
        word = lambda k: words[s, k].astype(jnp.int32)

        @pl.when(word(0) > 0)
        def _():
            ax, ay, az, hx, hy, hz = (word(k) for k in range(1, 7))
            covered = (row < hy) & (lane >= az) & (lane < az + hz)
            here = pl.ds(ay, edge)

            @pl.loop(0, lax.shift_right_logical(hx + groups - 1, 2))
            def _(tile):
                data = received[s, pl.ds(pl.multiple_of(tile * edge, edge), edge), :]
                for g in range(groups):
                    i = tile * groups + g
                    x = ax + i
                    moved = pltpu.roll(data, lax.rem(az + lanes - g * edge, lanes), 1)
                    change = jnp.where(covered & (i < hx), moved - coarse[x, here, :], 0.0)
                    source[x, here, :] = source[x, here, :] + change

    @pl.loop(0, planes // 2)
    def _(k):
        for half in range(2):
            y_low[k, half * HALO : half * HALO + HALO, :] = source[2 * k + half, 0:HALO, :]
            y_high[k, half * HALO : half * HALO + HALO, :] = source[2 * k + half, height - HALO : height, :]


def deposit(received, coarse):
    planes, height, lanes = coarse.shape
    face = jax.ShapeDtypeStruct((planes // 2, 2 * HALO, lanes), F32)
    vmem = pl.BlockSpec(memory_space=pltpu.VMEM)
    return pl.pallas_call(
        deposit_kernel,
        out_shape=[jax.ShapeDtypeStruct(coarse.shape, F32), face, face],
        in_specs=[vmem, vmem],
        out_specs=[vmem, vmem, vmem],
        scratch_shapes=[pltpu.SMEM((received.shape[0], lanes), F32), pltpu.SemaphoreType.DMA],
        compiler_params=pltpu.CompilerParams(vmem_limit_bytes=32 << 20),
        name="deposit",
    )(received, coarse)


def sweep_kernel(slabs, pencils, place, source, y_low, y_high, x_low, x_high, potential, gradient,
                 q1, q2, q3, q4, sems):
    step = pl.program_id(0)
    steps = pl.num_programs(0)
    planes, height, lanes = source.shape
    first, last = place[0] == 0, place[0] == slabs - 1
    left, right = place[1] == 0, place[1] == pencils - 1
    top = HALO + planes
    base = 2 * HALO
    window = pl.ds(HALO, height + 2 * HALO)
    below = pl.ds(HALO - 1, height + 2 * HALO)
    above = pl.ds(HALO + 1, height + 2 * HALO)

    def chunk(c):
        start = c * STEP if isinstance(c, int) else pl.multiple_of(c * STEP, STEP)
        return pltpu.make_async_copy(
            source.at[pl.ds(start, STEP)],
            q1.at[pl.ds(HALO + start, STEP), pl.ds(base, height), :],
            sems.at[c],
        )

    row = lax.broadcasted_iota(jnp.int32, (8, lanes), 0)
    keep_low = jnp.where(left & (row < HALO), 0.0, 1.0)
    keep_high = jnp.where(right & (row >= HALO), 0.0, 1.0)
    lane = lax.broadcasted_iota(jnp.int32, (height, lanes), 1)

    @pl.when(step == 0)
    def _():
        for c in range(planes // STEP):
            chunk(c).start()

        @pl.loop(0, planes // 2)
        def _(k):
            low = jnp.where(left, 0.0, y_low[k])
            high = jnp.where(right, 0.0, y_high[k])
            for half in range(2):
                x = HALO + 2 * k + half
                q1[x, HALO:base, :] = low[half * HALO : half * HALO + HALO]
                q1[x, base + height : base + height + HALO, :] = high[half * HALO : half * HALO + HALO]

        zero = jnp.zeros((height + 2 * HALO, lanes), F32)
        for i in range(HALO):
            for edge, x, face in ((first, i, x_low), (last, top + i, x_high)):
                value = jnp.where(edge, 0.0, face[i])
                q1[x, HALO : HALO + 8, :] = value[:8] * keep_low
                q1[x, HALO + 8 : height + HALO, :] = value[8:height]
                q1[x, height + HALO : height + 2 * HALO + HALO, :] = value[height:] * keep_high
                for q in (q2, q3, q4):
                    q[x, window, :] = zero
        chunk(0).wait()

    @pl.when(step < steps - 1)
    def _():
        chunk(step + 1).wait()

    def sides(value):
        lane_here = lax.broadcasted_iota(jnp.int32, value.shape, 1)
        down = jnp.where(lane_here == 0, 0.0, pltpu.roll(value, 1, 1))
        up = jnp.where(lane_here == lanes - 1, 0.0, pltpu.roll(value, lanes - 1, 1))
        return down, up

    def sweep(old, new, low, high):
        def body(x, carry):
            before, here = carry
            after = old[x + 1, window, :]
            down, up = sides(here)
            around = (before + after) + (old[x, below, :] + old[x, above, :]) + (down + up)
            value = q1[x, window, :] + (3.0 * here + around) * (1.0 / 9.0)
            new[x, HALO : HALO + 8, :] = value[:8] * keep_low
            new[x, HALO + 8 : height + HALO, :] = value[8:height]
            new[x, height + HALO : height + 2 * HALO + HALO, :] = value[height:] * keep_high
            return here, after

        lax.fori_loop(low, high, body, (old[low - 1, window, :], old[low, window, :]))

    for k, (old, new) in enumerate(((q1, q2), (q2, q3), (q3, q4))):
        start = jnp.where(step == 0, jnp.where(first, HALO, 1 + k), 7 - k + STEP * step)
        stop = jnp.minimum(15 - k + STEP * step, jnp.where(last, top, top + HALO - 1 - k))
        sweep(old, new, start, stop)

    own = pl.ds(base, height)

    def finish(j, carry):
        before, here = carry
        x = HALO + STEP * step + j
        after = q4[x + 1, own, :]
        down, up = sides(here)
        potential[j] = here * (1.0 / 9.0)
        gradient[0, j] = (after - before) * (0.5 / 9.0)
        gradient[1, j] = (q4[x, pl.ds(base + 1, height), :] - q4[x, pl.ds(base - 1, height), :]) * (0.5 / 9.0)
        gradient[2, j] = (up - down) * (0.5 / 9.0)
        return here, after

    x0 = HALO + STEP * step
    lax.fori_loop(0, STEP, finish, (q4[x0 - 1, own, :], q4[x0, own, :]))


def sweeps(place, source, y_low, y_high, x_low, x_high, slabs, pencils):
    planes, height, lanes = source.shape
    whole = lambda a: pl.BlockSpec(a.shape, lambda i, place: (0,) * a.ndim)
    field = pltpu.VMEM((planes + 2 * HALO, height + 4 * HALO, lanes), F32)
    return pl.pallas_call(
        functools.partial(sweep_kernel, slabs, pencils),
        out_shape=[
            jax.ShapeDtypeStruct(source.shape, F32),
            jax.ShapeDtypeStruct((3,) + source.shape, F32),
        ],
        grid_spec=pltpu.PrefetchScalarGridSpec(
            num_scalar_prefetch=1,
            grid=(planes // STEP,),
            in_specs=[pl.BlockSpec(memory_space=pl.ANY)] + [whole(a) for a in (y_low, y_high, x_low, x_high)],
            out_specs=[
                pl.BlockSpec((STEP, height, lanes), lambda i, place: (i, 0, 0)),
                pl.BlockSpec((3, STEP, height, lanes), lambda i, place: (0, i, 0, 0)),
            ],
            scratch_shapes=[field, field, field, field, pltpu.SemaphoreType.DMA((planes // STEP,))],
        ),
        compiler_params=pltpu.CompilerParams(
            dimension_semantics=("arbitrary",), vmem_limit_bytes=48 << 20
        ),
        name="sweeps",
    )(place, source, y_low, y_high, x_low, x_high)


def ring(values, axis, count):
    up = [(i, (i + 1) % count) for i in range(count)]
    down = [((i + 1) % count, i) for i in range(count)]
    low, high = values
    return lax.ppermute(high, axis, up), lax.ppermute(low, axis, down)


def on_device(fine, coarse, anchor, extent, owner, count):
    slabs, pencils = lax.axis_size("slab"), lax.axis_size("pencil")
    meta = jnp.concatenate(
        [anchor.reshape(-1), extent.reshape(-1), owner.reshape(-1), count.reshape(-1)]
    )
    sent = average(fine, meta, slabs)
    received = lax.all_to_all(sent, "slab", split_axis=0, concat_axis=0, tiled=True)
    source, y_low, y_high = deposit(received, coarse)
    planes, height, lanes = source.shape
    y_low, y_high = ring((y_low, y_high), "pencil", pencils)

    def face(at):
        near = slice(at // 2, at // 2 + HALO // 2)
        return jnp.concatenate(
            [y_low[near].reshape(HALO, HALO, lanes), source[at : at + HALO],
             y_high[near].reshape(HALO, HALO, lanes)],
            axis=1,
        )

    x_low, x_high = ring((face(0), face(planes - HALO)), "slab", slabs)
    place = jnp.stack([lax.axis_index("slab"), lax.axis_index("pencil")]).astype(jnp.int32)
    potential, gradient = sweeps(place, source, y_low, y_high, x_low, x_high, slabs, pencils)
    return potential, gradient


def solution(mesh):
    in_specs = (
        P("slab", "pencil", None, None, None, None),
        P("slab", "pencil", None),
        P("slab", "pencil", None, None),
        P("slab", "pencil", None, None),
        P("slab", "pencil", None, None),
        P("slab", "pencil"),
    )
    out_specs = (P("slab", "pencil", None), P(None, "slab", "pencil", None))
    return jax.shard_map(
        on_device, mesh=mesh, in_specs=in_specs, out_specs=out_specs, check_vma=False
    )
```

profile of v0, /device:TPU:0, one launch (start us, length us, event | category | flops | bytes accessed | tf_op | source)
XLA Modules:
  0.0 111.2 jit_solution(10146765267960247318)
XLA Ops:
  1.3 0.8 copy.10
  2.0 0.1 reshape.28
  2.1 0.8 copy.11
  2.9 0.1 reshape.29
  3.0 0.7 pad_add_fusion.1.meta
  3.7 0.0 copy-start
  3.7 5.8 %copy-done = f32[1,1,8,64,64,64]{5,4,3,2,1,0:T(8,128)S(1)} copy-done((f32[1,1,8,64,64,64]{5,4,3,2,1,0:T(8,128)S(1)}, f32[1,1,8,64,64,64]{5,4,3,2,1,0:T(8,128)}, u32[]{:S(2)}) %copy-start) | copy-done | bytes 8388632
  9.5 4.6 %average.1 = f32[16,264,128]{2,1,0:T(8,128)S(1)} custom-call(s32[57]{0:T(128)S(1)} %pad_add_fusion.1.meta, f32[1,1,8,64,64,64]{5,4,3,2,1,0:T(8,128)S(1)} %copy-done), custom_call_target="tpu_custom_call" | custom-call | tf_op jit(solution)/shard_map/average/pallas_call | solution.py:84
  14.0 0.0 copy-start.1
  14.0 37.3 %all_to_all.5.received = f32[16,264,128]{2,1,0:T(8,128)S(1)} all-to-all(f32[16,264,128]{2,1,0:T(8,128)S(1)} %average.1), channel_id=1, replica_groups=mesh['slab'=16,'pencil'=8] {'slab'}, dimensions={0} | all-to-all | bytes 4325376 | tf_op jit(solution)/shard_map/all_to_all | solution.py:299
  51.4 0.0 copy-done.1
  51.4 2.3 %deposit.1 = (f32[96,64,128]{2,1,0:T(8,128)S(1)}, f32[48,8,128]{2,1,0:T(8,128)S(1)}, f32[48,8,128]{2,1,0:T(8,128)S(1)}) custom-call(f32[16,264,128]{2,1,0:T(8,128)S(1)} %all_to_all.5.received, f32[96,64,128]{2,1,0:T(8,128)S(1)} %copy-done.1), custom_call_target="tpu_custom_call" | custom-call | tf_op jit(solution)/shard_map/deposit/pallas_call | solution.py:151
  53.7 1.8 %collective-permute-start = (f32[48,8,128]{2,1,0:T(8,128)S(1)}, f32[48,8,128]{2,1,0:T(8,128)S(1)}, u32[]{:S(2)}, u32[]{:S(2)}) collective-permute-start(f32[48,8,128]{2,1,0:T(8,128)S(1)} %get-tuple-element.6), channel_id=1, source_target_pairs={{0,1},{1,2},{2,3},{3,4},{4,5},{5,6},{6,7},{7,0},{8,9},{9,10},{10,1... | collective-permute-start | bytes 589832 | tf_op jit(solution)/shard_map/ppermute | solution.py:290
  55.5 2.2 %collective-permute-start.1 = (f32[48,8,128]{2,1,0:T(8,128)S(1)}, f32[48,8,128]{2,1,0:T(8,128)S(1)}, u32[]{:S(2)}, u32[]{:S(2)}) collective-permute-start(f32[48,8,128]{2,1,0:T(8,128)S(1)} %get-tuple-element.7), channel_id=1, source_target_pairs={{1,0},{2,1},{3,2},{4,3},{5,4},{6,5},{7,6},{0,7},{9,8},{10,9},{11,1... | collective-permute-start | bytes 589832 | tf_op jit(solution)/shard_map/ppermute | solution.py:290
  57.7 3.3 %collective-permute-done.y_low = f32[48,8,128]{2,1,0:T(8,128)S(1)} collective-permute-done((f32[48,8,128]{2,1,0:T(8,128)S(1)}, f32[48,8,128]{2,1,0:T(8,128)S(1)}, u32[]{:S(2)}, u32[]{:S(2)}) %collective-permute-start) | collective-permute-done | bytes 196640 | tf_op jit(solution)/shard_map/ppermute | solution.py:290
  61.0 0.0 collective-permute-done.1.y_high
  61.1 0.7 pad_maximum_fusion
  61.7 1.9 %collective-permute-start.2 = (f32[4,72,128]{2,1,0:T(8,128)}, f32[4,72,128]{2,1,0:T(8,128)}, u32[]{:S(2)}, u32[]{:S(2)}) collective-permute-start(f32[4,72,128]{2,1,0:T(8,128)} %pad_maximum_fusion), channel_id=1, source_target_pairs={{0,8},{8,16},{16,24},{24,32},{32,40},{40,48},{48,56},{56,64},{64,7... | collective-permute-start | bytes 442376 | tf_op jit(solution)/shard_map/ppermute | solution.py:290
  63.6 0.7 pad_maximum_fusion.1
  64.3 3.5 %collective-permute-start.3 = (f32[4,72,128]{2,1,0:T(8,128)}, f32[4,72,128]{2,1,0:T(8,128)}, u32[]{:S(2)}, u32[]{:S(2)}) collective-permute-start(f32[4,72,128]{2,1,0:T(8,128)} %pad_maximum_fusion.1), channel_id=1, source_target_pairs={{8,0},{16,8},{24,16},{32,24},{40,32},{48,40},{56,48},{64,56},{72,6... | collective-permute-start | bytes 442376 | tf_op jit(solution)/shard_map/ppermute | solution.py:290
  67.8 0.1 pad_add_fusion.place
  67.8 3.8 %collective-permute-done.2.x_low = f32[4,72,128]{2,1,0:T(8,128)} collective-permute-done((f32[4,72,128]{2,1,0:T(8,128)}, f32[4,72,128]{2,1,0:T(8,128)}, u32[]{:S(2)}, u32[]{:S(2)}) %collective-permute-start.2) | collective-permute-done | bytes 147488 | tf_op jit(solution)/shard_map/ppermute | solution.py:290
  71.6 0.0 collective-permute-done.3.x_high
  71.6 39.6 %sweeps.1 = (f32[96,64,128]{2,1,0:T(8,128)}, f32[3,96,64,128]{3,2,1,0:T(8,128)}) custom-call(s32[2]{0:T(128)S(1)} %pad_add_fusion.place, f32[96,64,128]{2,1,0:T(8,128)S(1)} %get-tuple-element.5.source, f32[48,8,128]{2,1,0:T(8,128)S(1)} %collective-permute-done.y_low, f32[48,8,128]{2,1,0:T(8,128)S(1)} %collective-permute-done.1.y_high, ...), custom_call_target="tpu_custom_call" | custom-call | tf_op jit(solution)/shard_map/sweeps/pallas_call | solution.py:263
  (3 shorter events, 0.0 us)
Async XLA Ops:
  3.7 5.8 %copy-start = (f32[1,1,8,64,64,64]{5,4,3,2,1,0:T(8,128)S(1)}, f32[1,1,8,64,64,64]{5,4,3,2,1,0:T(8,128)}, u32[]{:S(2)}) copy-start(f32[1,1,8,64,64,64]{5,4,3,2,1,0:T(8,128)} %fine.1) | copy-start | bytes 25165828
  14.0 37.3 %copy-start.1 = (f32[96,64,128]{2,1,0:T(8,128)S(1)}, f32[96,64,128]{2,1,0:T(8,128)}, u32[]{:S(2)}) copy-start(f32[96,64,128]{2,1,0:T(8,128)} %coarse.1) | copy-start | bytes 9437188
  53.7 7.3 %collective-permute-start = (f32[48,8,128]{2,1,0:T(8,128)S(1)}, f32[48,8,128]{2,1,0:T(8,128)S(1)}, u32[]{:S(2)}, u32[]{:S(2)}) collective-permute-start(f32[48,8,128]{2,1,0:T(8,128)S(1)} %get-tuple-element.6), channel_id=1, source_target_pairs={{0,1},{1,2},{2,3},{3,4},{4,5},{5,6},{6,7},{7,0},{8,9},{9,10},{10,1... | collective-permute-start | bytes 589832 | tf_op jit(solution)/shard_map/ppermute | solution.py:290
  55.5 5.6 %collective-permute-start.1 = (f32[48,8,128]{2,1,0:T(8,128)S(1)}, f32[48,8,128]{2,1,0:T(8,128)S(1)}, u32[]{:S(2)}, u32[]{:S(2)}) collective-permute-start(f32[48,8,128]{2,1,0:T(8,128)S(1)} %get-tuple-element.7), channel_id=1, source_target_pairs={{1,0},{2,1},{3,2},{4,3},{5,4},{6,5},{7,6},{0,7},{9,8},{10,9},{11,1... | collective-permute-start | bytes 589832 | tf_op jit(solution)/shard_map/ppermute | solution.py:290
  61.7 9.9 %collective-permute-start.2 = (f32[4,72,128]{2,1,0:T(8,128)}, f32[4,72,128]{2,1,0:T(8,128)}, u32[]{:S(2)}, u32[]{:S(2)}) collective-permute-start(f32[4,72,128]{2,1,0:T(8,128)} %pad_maximum_fusion), channel_id=1, source_target_pairs={{0,8},{8,16},{16,24},{24,32},{32,40},{40,48},{48,56},{56,64},{64,7... | collective-permute-start | bytes 442376 | tf_op jit(solution)/shard_map/ppermute | solution.py:290
  64.3 7.3 %collective-permute-start.3 = (f32[4,72,128]{2,1,0:T(8,128)}, f32[4,72,128]{2,1,0:T(8,128)}, u32[]{:S(2)}, u32[]{:S(2)}) collective-permute-start(f32[4,72,128]{2,1,0:T(8,128)} %pad_maximum_fusion.1), channel_id=1, source_target_pairs={{8,0},{16,8},{24,16},{32,24},{40,32},{48,40},{56,48},{64,56},{72,6... | collective-permute-start | bytes 442376 | tf_op jit(solution)/shard_map/ppermute | solution.py:290
where the time goes:
time: 113 us; the launch traced here: 111 us
  Pallas kernels  46.5 us (41%)
  blocking collectives  37.3 us (33%)
  starting transfers between devices  9.33 us (8%)
  local copies, waits for them, and re-layouts  7.47 us (7%)
  waiting for transfers between devices  7.09 us (6%)
  other arithmetic  2.17 us (2%)
  between operations  1.32 us (1%)
    pallas_call x1, Pallas kernels, sweeps(): pl.pallas_call(functools.partial(sweep_kernel, slabs, pencils), out_shape...  39.6 us
    all_to_all x1, blocking collectives, on_device(): lax.all_to_all(sent, 'slab', split_axis=0, concat_axis=0, tiled=True)  37.3 us
    ppermute x4, starting transfers between devices, ring(): return (lax.ppermute(high, axis, up), lax.ppermute(low, axis, down))  9.33 us
    unnamed x6, local copies, waits for them, and re-layouts  7.29 us
    ppermute x4, waiting for transfers between devices, ring(): return (lax.ppermute(high, axis, up), lax.ppermute(low, axis, down))  7.09 us
    pallas_call x1, Pallas kernels, average(): pl.pallas_call(average_kernel, out_shape=jax.ShapeDtypeStruct((slabs, row...  4.56 us
    pallas_call x1, Pallas kernels, deposit(): pl.pallas_call(deposit_kernel, out_shape=[jax.ShapeDtypeStruct(coarse.sha...  2.34 us
  transfers between devices with their start and end apart: 4, of which 2 were waited for; matrix products, arithmetic and copies ran while one was open for 1% of the time, Pallas kernels for 0%

commit v1 on v0

v1 whole, which is shorter than its diff:
```python
import functools

import jax
import jax.numpy as jnp
from jax import lax
from jax.experimental import pallas as pl
from jax.experimental.pallas import tpu as pltpu
from jax.sharding import PartitionSpec as P

HALO = 4
META_ROWS = 8
STEP = 8
BASE = 8
F32 = jnp.float32


def average_kernel(anchor, extent, owners, count, fine, sent, cells, packed, blank, in_sems, out_sem, blank_sem):
    slots, fine_edge = cells.shape[:2]
    rows = packed.shape[1] - META_ROWS
    edge = fine_edge // 2
    lanes = packed.shape[2]
    groups = lanes // edge
    tiles = edge // groups
    parts = in_sems.shape[1]
    share = fine_edge // parts

    def load(p, part):
        here = pl.ds(part * share, share)
        return pltpu.make_async_copy(fine.at[0, 0, p, here], cells.at[p, here], in_sems.at[p, part])

    def store(p):
        return pltpu.make_async_copy(packed.at[p], sent.at[owners[0, 0, 0, p]], out_sem)

    def clear():
        return pltpu.make_async_copy(blank, sent.at[:, pl.ds(rows, META_ROWS), :], blank_sem)

    for p in range(slots):
        for part in range(parts):
            load(p, part).start()
    blank[...] = jnp.zeros_like(blank)
    clear().start()
    lane = lax.broadcasted_iota(jnp.int32, (META_ROWS, lanes), 1)
    source_lane = lax.broadcasted_iota(jnp.int32, (fine_edge, lanes), 0)
    target_lane = lax.broadcasted_iota(jnp.int32, (fine_edge, lanes), 1)

    @pl.loop(0, slots)
    def _(p):
        for part in range(parts):
            load(p, part).wait()
        total = jnp.zeros((rows, lanes), F32)
        for g in range(groups):
            pieces = [
                cells[p, pl.ds(2 * g + dx, tiles, stride=2 * groups), pl.ds(dy, edge, stride=2), :]
                for dx in range(2) for dy in range(2)
            ]
            part = ((pieces[0] + pieces[1]) + (pieces[2] + pieces[3])).reshape(rows, fine_edge)
            high = part.astype(jnp.bfloat16)
            low = (part - high.astype(F32)).astype(jnp.bfloat16)
            gather = jnp.where(target_lane == g * edge + source_lane // 2, 0.125, 0.0).astype(jnp.bfloat16)
            total = total + jnp.dot(high, gather, preferred_element_type=F32)
            total = total + jnp.dot(low, gather, preferred_element_type=F32)
        packed[p, :rows, :] = total
        alive = (p < count[0, 0]).astype(jnp.int32)
        words = jnp.where(lane == 0, alive, 0)
        for d in range(3):
            words = jnp.where(lane == 1 + d, anchor[0, d, 0, p], words)
            words = jnp.where(lane == 4 + d, lax.shift_right_logical(extent[0, d, 0, p], 1), words)
        packed[p, pl.ds(rows, META_ROWS), :] = words.astype(F32)
        pl.when(p == 0)(lambda: clear().wait())
        store(p).start()

    @pl.loop(0, slots)
    def _(p):
        store(p).wait()


def average(fine, anchor, extent, owner, count, slabs):
    by_component = lambda a: jnp.transpose(a, (0, 3, 1, 2))
    slots, fine_edge = fine.shape[2], fine.shape[3]
    edge = fine_edge // 2
    rows = edge * edge * edge // 128
    smem = pl.BlockSpec(memory_space=pltpu.SMEM)
    return pl.pallas_call(
        average_kernel,
        out_shape=jax.ShapeDtypeStruct((slabs, rows + META_ROWS, 128), F32),
        in_specs=[smem, smem, smem, smem, pl.BlockSpec(memory_space=pl.ANY)],
        out_specs=pl.BlockSpec(memory_space=pl.ANY),
        scratch_shapes=[
            pltpu.VMEM(fine.shape[2:], F32),
            pltpu.VMEM((slots, rows + META_ROWS, 128), F32),
            pltpu.VMEM((slabs, META_ROWS, 128), F32),
            pltpu.SemaphoreType.DMA((slots, 2)),
            pltpu.SemaphoreType.DMA,
            pltpu.SemaphoreType.DMA,
        ],
        compiler_params=pltpu.CompilerParams(vmem_limit_bytes=56 << 20),
        name="average",
    )(by_component(anchor), by_component(extent), by_component(owner), count, fine)


def deposit_kernel(received, coarse, source, y_low, y_high, words, sem):
    slabs, all_rows, lanes = received.shape
    rows = all_rows - META_ROWS
    edge = 32
    groups = lanes // edge
    planes, height, _ = source.shape
    for s in range(slabs):
        pltpu.make_async_copy(received.at[s, rows], words.at[s], sem).start()
    source[...] = jnp.zeros_like(source)
    for s in range(slabs):
        pltpu.make_async_copy(received.at[s, rows], words.at[s], sem).wait()
    row = lax.broadcasted_iota(jnp.int32, (edge, lanes), 0)
    lane = lax.broadcasted_iota(jnp.int32, (edge, lanes), 1)

    @pl.loop(0, slabs)
    def _(s):
        word = lambda k: words[s, k].astype(jnp.int32)

        @pl.when(word(0) > 0)
        def _():
            ax, ay, az, hx, hy, hz = (word(k) for k in range(1, 7))
            covered = (row < hy) & (lane >= az) & (lane < az + hz)
            here = pl.ds(ay, edge)

            @pl.loop(0, lax.shift_right_logical(hx + groups - 1, 2))
            def _(tile):
                data = received[s, pl.ds(pl.multiple_of(tile * edge, edge), edge), :]
                for g in range(groups):
                    i = tile * groups + g
                    x = ax + i
                    moved = pltpu.roll(data, lax.rem(az + lanes - g * edge, lanes), 1)
                    change = jnp.where(covered & (i < hx), moved - coarse[x, here, :], 0.0)
                    source[x, here, :] = source[x, here, :] + change

    @pl.loop(0, planes // 2)
    def _(k):
        for half in range(2):
            y_low[k, half * HALO : half * HALO + HALO, :] = source[2 * k + half, 0:HALO, :]
            y_high[k, half * HALO : half * HALO + HALO, :] = source[2 * k + half, height - HALO : height, :]


def deposit(received, coarse):
    planes, height, lanes = coarse.shape
    face = jax.ShapeDtypeStruct((planes // 2, 2 * HALO, lanes), F32)
    vmem = pl.BlockSpec(memory_space=pltpu.VMEM)
    return pl.pallas_call(
        deposit_kernel,
        out_shape=[jax.ShapeDtypeStruct(coarse.shape, F32), face, face],
        in_specs=[vmem, vmem],
        out_specs=[vmem, vmem, vmem],
        scratch_shapes=[pltpu.SMEM((received.shape[0], lanes), F32), pltpu.SemaphoreType.DMA],
        compiler_params=pltpu.CompilerParams(vmem_limit_bytes=32 << 20),
        name="deposit",
    )(received, coarse)


def sweep_kernel(slabs, pencils, place, source, y_low, y_high, x_low, x_high, potential, gradient,
                 q1, q2, q3, q4, potential_out, gradient_out, sems):
    planes, height, lanes = source.shape
    rows = height // 8
    steps = planes // STEP
    first, last = place[0] == 0, place[0] == slabs - 1
    left, right = place[1] == 0, place[1] == pencils - 1
    row = lax.broadcasted_iota(jnp.int32, (8, lanes), 0)
    lane = lax.broadcasted_iota(jnp.int32, (8, lanes), 1)
    keep = jnp.where((right & (row < HALO)) | (left & (row >= HALO)), 0.0, 1.0)

    def send(i):
        here = pl.ds(i * STEP, STEP)
        copies = [pltpu.make_async_copy(potential_out.at[here], potential.at[here], sems.at[0])]
        for d in range(3):
            copies.append(pltpu.make_async_copy(gradient_out.at[d, here], gradient.at[d, here], sems.at[1 + d]))
        return copies

    def comb(t):
        return pl.ds(t, 8, stride=rows)

    def load(field, x):
        return tuple(field[x, t] for t in range(rows + 1))

    def unpack(c):
        for j in range(STEP):
            x = c * STEP + j
            for t in range(rows):
                q1[BASE + x, t] = source[x, comb(t), :]

    @pl.loop(0, planes // 2)
    def _(k):
        low, high = y_low[k], y_high[k]
        q1[BASE + 2 * k, rows] = jnp.where(row < HALO, high, pltpu.roll(low, HALO, 0)) * keep
        q1[BASE + 2 * k + 1, rows] = jnp.where(row < HALO, pltpu.roll(high, HALO, 0), low) * keep

    for i in range(HALO):
        for edge, x, face in ((first, BASE - HALO + i, x_low), (last, BASE + planes + i, x_high)):
            scale = jnp.where(edge, 0.0, 1.0)
            for t in range(rows):
                q1[x, t] = face[i, comb(HALO + t), :] * scale
            ends = jnp.where(row < HALO, face[i, 0:8, :], face[i, height : height + 8, :])
            q1[x, rows] = pltpu.roll(ends, HALO, 0) * (keep * scale)

    def along_z(value):
        down = jnp.where(lane == 0, 0.0, pltpu.roll(value, 1, 1))
        up = jnp.where(lane == lanes - 1, 0.0, pltpu.roll(value, lanes - 1, 1))
        return down, up

    def along_y(here):
        ends = here[rows]
        below = (pltpu.roll(jnp.where(row == 7, ends, here[rows - 1]), 1, 0),) + here[: rows - 1]
        above = here[1:rows] + (pltpu.roll(jnp.where(row == 0, ends, here[0]), 7, 0),)
        below += (pltpu.roll(jnp.where(row == 7, here[rows - 1], ends), 1, 0),)
        above += (pltpu.roll(jnp.where(row == 0, here[0], ends), 7, 0),)
        return below, above

    def sweep(old, new, start):
        before, here = load(old, start - 1), load(old, start)
        for j in range(STEP):
            x = start + j
            after = load(old, x + 1)
            below, above = along_y(here)
            for t in range(rows + 1):
                down, up = along_z(here[t])
                around = (before[t] + after[t]) + (below[t] + above[t]) + (down + up)
                value = q1[x, t] + (3.0 * here[t] + around) * (1.0 / 9.0)
                value = value * keep if t == rows else value
                new[x, t] = value
            before, here = here, after
        return value

    def clear(field, start):
        for i in range(HALO):
            field[start + i] = jnp.zeros((rows + 1, 8, lanes), F32)

    fields = ((q1, q2), (q2, q3), (q3, q4))
    unpack(0)
    for k, (old, new) in enumerate(fields):
        ends = sweep(old, new, BASE - 5 - k)
        pl.when(first)(functools.partial(clear, new, BASE - HALO))

    def advance(i, ends):
        pl.when(i < steps - 1)(lambda: unpack(i + 1))
        for k, (old, new) in enumerate(fields):
            next_ends = sweep(old, new, BASE + 3 - k + i * STEP)
            pl.when(last & (i == steps - 1))(functools.partial(clear, new, BASE + planes))
        x0 = BASE + i * STEP
        before, here = load(q4, x0 - 1), load(q4, x0)[:rows] + (ends,)
        for j in range(STEP):
            x = i * STEP + j
            after = load(q4, x0 + j + 1)
            below, above = along_y(here)
            for t in range(rows):
                down, up = along_z(here[t])
                potential_out[x, comb(t), :] = here[t] * (1.0 / 9.0)
                gradient_out[0, x, comb(t), :] = (after[t] - before[t]) * (0.5 / 9.0)
                gradient_out[1, x, comb(t), :] = (above[t] - below[t]) * (0.5 / 9.0)
                gradient_out[2, x, comb(t), :] = (up - down) * (0.5 / 9.0)
            before, here = here, after
        for copy in send(i):
            copy.start()
        return next_ends

    lax.fori_loop(0, steps, advance, ends)

    @pl.loop(0, steps)
    def _(i):
        for copy in send(i):
            copy.wait()


def sweeps(place, source, y_low, y_high, x_low, x_high, slabs, pencils):
    planes, height, lanes = source.shape
    field = pltpu.VMEM((BASE + planes + 2 * HALO, height // 8 + 1, 8, lanes), F32)
    vmem = pl.BlockSpec(memory_space=pltpu.VMEM)
    return pl.pallas_call(
        functools.partial(sweep_kernel, slabs, pencils),
        out_shape=[
            jax.ShapeDtypeStruct(source.shape, F32),
            jax.ShapeDtypeStruct((3,) + source.shape, F32),
        ],
        in_specs=[pl.BlockSpec(memory_space=pltpu.SMEM)] + [vmem] * 5,
        out_specs=[pl.BlockSpec(memory_space=pl.ANY)] * 2,
        scratch_shapes=[
            field, field, field, field,
            pltpu.VMEM(source.shape, F32),
            pltpu.VMEM((3,) + source.shape, F32),
            pltpu.SemaphoreType.DMA((4,)),
        ],
        compiler_params=pltpu.CompilerParams(vmem_limit_bytes=44 << 20),
        name="sweeps",
    )(place, source, y_low, y_high, x_low, x_high)


def ring(values, axis, count):
    up = [(i, (i + 1) % count) for i in range(count)]
    down = [((i + 1) % count, i) for i in range(count)]
    low, high = values
    return lax.ppermute(high, axis, up), lax.ppermute(low, axis, down)


def on_device(fine, coarse, anchor, extent, owner, count):
    slabs, pencils = lax.axis_size("slab"), lax.axis_size("pencil")
    sent = average(fine, anchor, extent, owner, count, slabs)
    received = lax.all_to_all(sent, "slab", split_axis=0, concat_axis=0, tiled=True)
    source, y_low, y_high = deposit(received, coarse)
    planes, height, lanes = source.shape
    y_low, y_high = ring((y_low, y_high), "pencil", pencils)

    def face(at):
        near = slice(at // 2, at // 2 + HALO // 2)
        return jnp.concatenate(
            [y_low[near].reshape(HALO, HALO, lanes), source[at : at + HALO],
             y_high[near].reshape(HALO, HALO, lanes)],
            axis=1,
        )

    x_low, x_high = ring((face(0), face(planes - HALO)), "slab", slabs)
    place = jnp.stack([lax.axis_index("slab"), lax.axis_index("pencil")]).astype(jnp.int32)
    potential, gradient = sweeps(place, source, y_low, y_high, x_low, x_high, slabs, pencils)
    return potential, gradient


def solution(mesh):
    in_specs = (
        P("slab", "pencil", None, None, None, None),
        P("slab", "pencil", None),
        P("slab", "pencil", None, None),
        P("slab", "pencil", None, None),
        P("slab", "pencil", None, None),
        P("slab", "pencil"),
    )
    out_specs = (P("slab", "pencil", None), P(None, "slab", "pencil", None))
    return jax.shard_map(
        on_device, mesh=mesh, in_specs=in_specs, out_specs=out_specs, check_vma=False
    )
```

time: 113 us -> 85.9 us (0.76)
  the two profiles are of different devices: /device:TPU:0 before, /device:TPU:1 now
where the time goes in v1:
time: 85.9 us; the launch traced here: 84.4 us
  blocking collectives  37 us (43%)
  Pallas kernels  25.9 us (30%)
  starting transfers between devices  9.95 us (12%)
  waiting for transfers between devices  8.71 us (10%)
  other arithmetic  1.43 us (2%)
  between operations  1.31 us (2%)
    all_to_all x1, blocking collectives, on_device(): lax.all_to_all(sent, 'slab', split_axis=0, concat_axis=0, tiled=True)  37 us
    pallas_call x1, Pallas kernels, sweeps(): pl.pallas_call(functools.partial(sweep_kernel, slabs, pencils), out_shape...  14.8 us
    ppermute x4, starting transfers between devices, ring(): return (lax.ppermute(high, axis, up), lax.ppermute(low, axis, down))  9.95 us
    ppermute x4, waiting for transfers between devices, ring(): return (lax.ppermute(high, axis, up), lax.ppermute(low, axis, down))  8.71 us
    pallas_call x1, Pallas kernels, average(): pl.pallas_call(average_kernel, out_shape=jax.ShapeDtypeStruct((slabs, row...  7.96 us
    pallas_call x1, Pallas kernels, deposit(): pl.pallas_call(deposit_kernel, out_shape=[jax.ShapeDtypeStruct(coarse.sha...  3.15 us
  transfers between devices with their start and end apart: 4, of which 4 were waited for; matrix products, arithmetic and copies ran while one was open for 1% of the time, Pallas kernels for 0%

profile of v1, /device:TPU:1, one launch (start us, length us, event | category | flops | bytes accessed | tf_op | source)
XLA Modules:
  0.0 84.4 jit_solution(4376060937541601838)
XLA Ops:
  1.3 8.0 %average.1 = f32[16,264,128]{2,1,0:T(8,128)} custom-call(s32[1,3,1,8]{3,2,1,0:T(1,128)} %bitcast.13, s32[1,3,1,8]{3,2,1,0:T(1,128)} %bitcast.14, s32[1,1,1,8]{3,2,1,0:T(1,128)} %bitcast.15, s32[1,1]{1,0:T(1,128)S(6)} %copy.8.count, f32[1,1,8,64,64,64]{5,4,3,2,1,0:T(8,128)} %fine.1), custom_call_target="tpu_custom_call" | custom-call | tf_op jit(solution)/shard_map/average/pallas_call | solution.py:83
  9.2 0.0 copy-start
  9.3 37.0 %all_to_all.5.received = f32[16,264,128]{2,1,0:T(8,128)S(1)} all-to-all(f32[16,264,128]{2,1,0:T(8,128)} %average.1), channel_id=1, replica_groups=mesh['slab'=16,'pencil'=8] {'slab'}, dimensions={0} | all-to-all | bytes 4325376 | tf_op jit(solution)/shard_map/all_to_all | solution.py:302
  46.3 0.0 copy-done
  46.3 3.1 %deposit.1 = (f32[96,64,128]{2,1,0:T(8,128)S(1)}, f32[48,8,128]{2,1,0:T(8,128)S(1)}, f32[48,8,128]{2,1,0:T(8,128)S(1)}) custom-call(f32[16,264,128]{2,1,0:T(8,128)S(1)} %all_to_all.5.received, f32[96,64,128]{2,1,0:T(8,128)S(1)} %copy-done), custom_call_target="tpu_custom_call" | custom-call | tf_op jit(solution)/shard_map/deposit/pallas_call | solution.py:146
  49.4 5.2 %collective-permute-start = (f32[48,8,128]{2,1,0:T(8,128)S(1)}, f32[48,8,128]{2,1,0:T(8,128)S(1)}, u32[]{:S(2)}, u32[]{:S(2)}) collective-permute-start(f32[48,8,128]{2,1,0:T(8,128)S(1)} %get-tuple-element.6), channel_id=1, source_target_pairs={{0,1},{1,2},{2,3},{3,4},{4,5},{5,6},{6,7},{7,0},{8,9},{9,10},{10,1... | collective-permute-start | bytes 589832 | tf_op jit(solution)/shard_map/ppermute | solution.py:296
  54.6 0.0 collective-permute-start.1
  54.6 2.6 %collective-permute-done.y_low = f32[48,8,128]{2,1,0:T(8,128)S(1)} collective-permute-done((f32[48,8,128]{2,1,0:T(8,128)S(1)}, f32[48,8,128]{2,1,0:T(8,128)S(1)}, u32[]{:S(2)}, u32[]{:S(2)}) %collective-permute-start) | collective-permute-done | bytes 196640 | tf_op jit(solution)/shard_map/ppermute | solution.py:296
  57.2 2.5 %collective-permute-done.1.y_high = f32[48,8,128]{2,1,0:T(8,128)S(1)} collective-permute-done((f32[48,8,128]{2,1,0:T(8,128)S(1)}, f32[48,8,128]{2,1,0:T(8,128)S(1)}, u32[]{:S(2)}, u32[]{:S(2)}) %collective-permute-start.1) | collective-permute-done | bytes 196640 | tf_op jit(solution)/shard_map/ppermute | solution.py:296
  59.7 0.7 pad_maximum_fusion
  60.4 0.0 collective-permute-start.2
  60.4 0.7 pad_maximum_fusion.1
  61.0 4.8 %collective-permute-start.3 = (f32[4,72,128]{2,1,0:T(8,128)}, f32[4,72,128]{2,1,0:T(8,128)}, u32[]{:S(2)}, u32[]{:S(2)}) collective-permute-start(f32[4,72,128]{2,1,0:T(8,128)} %pad_maximum_fusion.1), channel_id=1, source_target_pairs={{8,0},{16,8},{24,16},{32,24},{40,32},{48,40},{56,48},{64,56},{72,6... | collective-permute-start | bytes 442376 | tf_op jit(solution)/shard_map/ppermute | solution.py:296
  65.8 0.1 pad_add_fusion.place
  65.9 3.1 %collective-permute-done.2.x_low = f32[4,72,128]{2,1,0:T(8,128)} collective-permute-done((f32[4,72,128]{2,1,0:T(8,128)}, f32[4,72,128]{2,1,0:T(8,128)}, u32[]{:S(2)}, u32[]{:S(2)}) %collective-permute-start.2) | collective-permute-done | bytes 147488 | tf_op jit(solution)/shard_map/ppermute | solution.py:296
  69.0 0.5 collective-permute-done.3.x_high
  69.5 14.8 %sweeps.1 = (f32[96,64,128]{2,1,0:T(8,128)}, f32[3,96,64,128]{3,2,1,0:T(8,128)}) custom-call(s32[2]{0:T(128)S(1)} %pad_add_fusion.place, f32[96,64,128]{2,1,0:T(8,128)S(1)} %get-tuple-element.5.source, f32[48,8,128]{2,1,0:T(8,128)S(1)} %collective-permute-done.y_low, f32[48,8,128]{2,1,0:T(8,128)S(1)} %collective-permute-done.1.y_high, ...), custom_call_target="tpu_custom_call" | custom-call | tf_op jit(solution)/shard_map/sweeps/pallas_call | solution.py:273
  (3 shorter events, 0.0 us)
Async XLA Ops:
  9.2 37.0 %copy-start = (f32[96,64,128]{2,1,0:T(8,128)S(1)}, f32[96,64,128]{2,1,0:T(8,128)}, u32[]{:S(2)}) copy-start(f32[96,64,128]{2,1,0:T(8,128)} %coarse.1) | copy-start | bytes 9437188
  49.4 7.8 %collective-permute-start = (f32[48,8,128]{2,1,0:T(8,128)S(1)}, f32[48,8,128]{2,1,0:T(8,128)S(1)}, u32[]{:S(2)}, u32[]{:S(2)}) collective-permute-start(f32[48,8,128]{2,1,0:T(8,128)S(1)} %get-tuple-element.6), channel_id=1, source_target_pairs={{0,1},{1,2},{2,3},{3,4},{4,5},{5,6},{6,7},{7,0},{8,9},{9,10},{10,1... | collective-permute-start | bytes 589832 | tf_op jit(solution)/shard_map/ppermute | solution.py:296
  54.6 5.1 %collective-permute-start.1 = (f32[48,8,128]{2,1,0:T(8,128)S(1)}, f32[48,8,128]{2,1,0:T(8,128)S(1)}, u32[]{:S(2)}, u32[]{:S(2)}) collective-permute-start(f32[48,8,128]{2,1,0:T(8,128)S(1)} %get-tuple-element.7), channel_id=1, source_target_pairs={{1,0},{2,1},{3,2},{4,3},{5,4},{6,5},{7,6},{0,7},{9,8},{10,9},{11,1... | collective-permute-start | bytes 589832 | tf_op jit(solution)/shard_map/ppermute | solution.py:296
  60.4 8.7 %collective-permute-start.2 = (f32[4,72,128]{2,1,0:T(8,128)}, f32[4,72,128]{2,1,0:T(8,128)}, u32[]{:S(2)}, u32[]{:S(2)}) collective-permute-start(f32[4,72,128]{2,1,0:T(8,128)} %pad_maximum_fusion), channel_id=1, source_target_pairs={{0,8},{8,16},{16,24},{24,32},{32,40},{40,48},{48,56},{56,64},{64,7... | collective-permute-start | bytes 442376 | tf_op jit(solution)/shard_map/ppermute | solution.py:296
  61.0 8.5 %collective-permute-start.3 = (f32[4,72,128]{2,1,0:T(8,128)}, f32[4,72,128]{2,1,0:T(8,128)}, u32[]{:S(2)}, u32[]{:S(2)}) collective-permute-start(f32[4,72,128]{2,1,0:T(8,128)} %pad_maximum_fusion.1), channel_id=1, source_target_pairs={{8,0},{16,8},{24,16},{32,24},{40,32},{48,40},{56,48},{64,56},{72,6... | collective-permute-start | bytes 442376 | tf_op jit(solution)/shard_map/ppermute | solution.py:296

commit v2 on v1

--- a/solution.py
+++ b/solution.py
@@ -11,10 +11,11 @@
 META_ROWS = 8
 STEP = 8
 BASE = 8
+GROUP = 4
 F32 = jnp.float32
 
 
-def average_kernel(anchor, extent, owners, count, fine, sent, cells, packed, blank, in_sems, out_sem, blank_sem):
+def average_kernel(slab, pencil, anchor, extent, owners, count, fine, sent, cells, packed, blank, in_sems, out_sem, blank_sem):
     slots, fine_edge = cells.shape[:2]
     rows = packed.shape[1] - META_ROWS
     edge = fine_edge // 2
@@ -74,7 +75,7 @@
         store(p).wait()
 
 
-def average(fine, anchor, extent, owner, count, slabs):
+def average(place, fine, anchor, extent, owner, count, slabs):
     by_component = lambda a: jnp.transpose(a, (0, 3, 1, 2))
     slots, fine_edge = fine.shape[2], fine.shape[3]
     edge = fine_edge // 2
@@ -83,7 +84,7 @@
     return pl.pallas_call(
         average_kernel,
         out_shape=jax.ShapeDtypeStruct((slabs, rows + META_ROWS, 128), F32),
-        in_specs=[smem, smem, smem, smem, pl.BlockSpec(memory_space=pl.ANY)],
+        in_specs=[smem] * 6 + [pl.BlockSpec(memory_space=pl.ANY)],
         out_specs=pl.BlockSpec(memory_space=pl.ANY),
         scratch_shapes=[
             pltpu.VMEM(fine.shape[2:], F32),
@@ -95,7 +96,7 @@
         ],
         compiler_params=pltpu.CompilerParams(vmem_limit_bytes=56 << 20),
         name="average",
-    )(by_component(anchor), by_component(extent), by_component(owner), count, fine)
+    )(*place, by_component(anchor), by_component(extent), by_component(owner), count, fine)
 
 
 def deposit_kernel(received, coarse, source, y_low, y_high, words, sem):
@@ -149,20 +150,109 @@
         in_specs=[vmem, vmem],
         out_specs=[vmem, vmem, vmem],
         scratch_shapes=[pltpu.SMEM((received.shape[0], lanes), F32), pltpu.SemaphoreType.DMA],
-        compiler_params=pltpu.CompilerParams(vmem_limit_bytes=32 << 20),
+        compiler_params=pltpu.CompilerParams(vmem_limit_bytes=4 << 20),
         name="deposit",
     )(received, coarse)
 
 
-def sweep_kernel(slabs, pencils, place, source, y_low, y_high, x_low, x_high, potential, gradient,
-                 q1, q2, q3, q4, potential_out, gradient_out, sems):
+def along_z(value):
+    lanes = value.shape[1]
+    lane = lax.broadcasted_iota(jnp.int32, value.shape, 1)
+    down = jnp.where(lane == 0, 0.0, pltpu.roll(value, 1, 1))
+    up = jnp.where(lane == lanes - 1, 0.0, pltpu.roll(value, lanes - 1, 1))
+    return down, up
+
+
+def z_terms(value):
+    lanes = value.shape[1]
+    lane = lax.broadcasted_iota(jnp.int32, value.shape, 1)
+    down = [None] + [jnp.where(lane < d, 0.0, pltpu.roll(value, d, 1)) for d in (1, 2, 3)]
+    up = [None] + [jnp.where(lane >= lanes - d, 0.0, pltpu.roll(value, lanes - d, 1)) for d in (1, 2, 3)]
+    outer = (lane == 0) | (lane == lanes - 1)
+    once = down[1] + up[1]
+    twice = (down[2] + up[2]) + jnp.where(outer, 1.0, 2.0) * value
+    thrice = (down[3] + up[3]) + (
+        jnp.where((lane == 0) | (lane == lanes - 2), 2.0, 3.0) * up[1]
+        + jnp.where((lane == 1) | (lane == lanes - 1), 2.0, 3.0) * down[1]
+    )
+    return (
+        value,
+        value + once * (1.0 / 3.0),
+        value + (once * (2.0 / 9.0) + twice * (1.0 / 27.0)),
+        (value + once * (1.0 / 9.0)) + (twice * (1.0 / 81.0) + thrice * (1.0 / 729.0)),
+    )
+
+
+def prepare_kernel(source, *fields):
+    planes, height, _ = source.shape
+    rows = height // 8
+
+    @pl.loop(0, planes // GROUP)
+    def _(k):
+        for j in range(GROUP):
+            for t in range(rows):
+                for field, term in zip(fields, z_terms(source[GROUP * k + j, pl.ds(t, 8, stride=rows), :])):
+                    field[GROUP * k + j, t] = term
+
+
+def prepare(source):
     planes, height, lanes = source.shape
-    rows = height // 8
+    field = jax.ShapeDtypeStruct((planes, height // 8, 8, lanes), F32)
+    vmem = pl.BlockSpec(memory_space=pltpu.VMEM)
+    return pl.pallas_call(
+        prepare_kernel,
+        out_shape=[field] * 4,
+        in_specs=[vmem],
+        out_specs=[vmem] * 4,
+        compiler_params=pltpu.CompilerParams(vmem_limit_bytes=4 << 20),
+        cost_estimate=pl.CostEstimate(flops=1 << 25, bytes_accessed=15 << 20, transcendentals=0),
+        name="prepare",
+    )(source)
+
+
+def y_ends(low, high, half):
+    row = lax.broadcasted_iota(jnp.int32, low.shape, 0)
+    if half == 0:
+        return jnp.where(row < HALO, high, pltpu.roll(low, HALO, 0))
+    return jnp.where(row < HALO, pltpu.roll(high, HALO, 0), low)
+
+
+def faces_kernel(field, y_low, y_high, x_low, x_high):
+    planes, rows, _, _ = field.shape
+    for face, start in ((x_low, 0), (x_high, planes - HALO)):
+        for i in range(HALO):
+            k, half = divmod(start + i, 2)
+            for t in range(rows):
+                face[i, t] = field[start + i, t]
+            face[i, rows] = y_ends(y_low[k], y_high[k], half)
+
+
+def faces(field, y_low, y_high):
+    face = jax.ShapeDtypeStruct((HALO, field.shape[1] + 1) + field.shape[2:], F32)
+    vmem = pl.BlockSpec(memory_space=pltpu.VMEM)
+    return pl.pallas_call(
+        faces_kernel,
+        out_shape=[face, face],
+        in_specs=[vmem] * 3,
+        out_specs=[vmem] * 2,
+        compiler_params=pltpu.CompilerParams(vmem_limit_bytes=4 << 20),
+        name="faces",
+    )(field, y_low, y_high)
+
+
+def sweep_kernel(inner, slabs, pencils, slab, pencil, f0, f1, f2, f3, y_low, y_high, *rest):
+    if inner:
+        potential, gradient, *rest = rest
+    else:
+        x_low, x_high, _, _, potential, gradient, *rest = rest
+    ends, v1, v2, v3, potential_out, gradient_out, sems, *rest = rest
+    fields = (f0, f1, f2, f3)
+    planes, rows, _, lanes = f0.shape
+    height = rows * 8
     steps = planes // STEP
-    first, last = place[0] == 0, place[0] == slabs - 1
-    left, right = place[1] == 0, place[1] == pencils - 1
+    first, last = slab[0] == 0, slab[0] == slabs - 1
+    left, right = pencil[0] == 0, pencil[0] == pencils - 1
     row = lax.broadcasted_iota(jnp.int32, (8, lanes), 0)
-    lane = lax.broadcasted_iota(jnp.int32, (8, lanes), 1)
     keep = jnp.where((right & (row < HALO)) | (left & (row >= HALO)), 0.0, 1.0)
 
     def send(i):
@@ -175,77 +265,87 @@
     def comb(t):
         return pl.ds(t, 8, stride=rows)
 
+    def set_ends(x, value):
+        for k, term in enumerate(z_terms(value)):
+            ends[k, BASE + x] = term
+
+    def set_y_faces(k):
+        low, high = y_low[k], y_high[k]
+        for half in range(2):
+            set_ends(2 * k + half, y_ends(low, high, half) * keep)
+
+    if inner:
+        @pl.loop(0, planes // 16)
+        def _(k):
+            for j in range(8):
+                set_y_faces(8 * k + j)
+    else:
+        for j in range(8):
+            set_y_faces(j)
+            set_y_faces(planes // 2 - 1 - j)
+        (beyond,) = rest
+        for i in range(HALO):
+            for edge, x, face in ((first, i - HALO, x_low), (last, planes + i, x_high)):
+                scale = jnp.where(edge, 0.0, 1.0)
+                for t in range(rows):
+                    for k, term in enumerate(z_terms(face[i, t] * scale)):
+                        beyond[k, x % (2 * HALO), t] = term
+                set_ends(x, face[i, rows] * (keep * scale))
+
+    def given(k, x):
+        if isinstance(x, int) and not 0 <= x < planes:
+            return tuple(beyond[k, x % (2 * HALO), t] for t in range(rows)) + (ends[k, BASE + x],)
+        return tuple(fields[k][x, t] for t in range(rows)) + (ends[k, BASE + x],)
+
     def load(field, x):
-        return tuple(field[x, t] for t in range(rows + 1))
-
-    def unpack(c):
-        for j in range(STEP):
-            x = c * STEP + j
-            for t in range(rows):
-                q1[BASE + x, t] = source[x, comb(t), :]
-
-    @pl.loop(0, planes // 2)
-    def _(k):
-        low, high = y_low[k], y_high[k]
-        q1[BASE + 2 * k, rows] = jnp.where(row < HALO, high, pltpu.roll(low, HALO, 0)) * keep
-        q1[BASE + 2 * k + 1, rows] = jnp.where(row < HALO, pltpu.roll(high, HALO, 0), low) * keep
-
-    for i in range(HALO):
-        for edge, x, face in ((first, BASE - HALO + i, x_low), (last, BASE + planes + i, x_high)):
-            scale = jnp.where(edge, 0.0, 1.0)
-            for t in range(rows):
-                q1[x, t] = face[i, comb(HALO + t), :] * scale
-            ends = jnp.where(row < HALO, face[i, 0:8, :], face[i, height : height + 8, :])
-            q1[x, rows] = pltpu.roll(ends, HALO, 0) * (keep * scale)
-
-    def along_z(value):
-        down = jnp.where(lane == 0, 0.0, pltpu.roll(value, 1, 1))
-        up = jnp.where(lane == lanes - 1, 0.0, pltpu.roll(value, lanes - 1, 1))
-        return down, up
+        return tuple(field[BASE + x, t] for t in range(rows + 1))
 
     def along_y(here):
-        ends = here[rows]
-        below = (pltpu.roll(jnp.where(row == 7, ends, here[rows - 1]), 1, 0),) + here[: rows - 1]
-        above = here[1:rows] + (pltpu.roll(jnp.where(row == 0, ends, here[0]), 7, 0),)
-        below += (pltpu.roll(jnp.where(row == 7, here[rows - 1], ends), 1, 0),)
-        above += (pltpu.roll(jnp.where(row == 0, here[0], ends), 7, 0),)
+        side = here[rows]
+        below = (pltpu.roll(jnp.where(row == 7, side, here[rows - 1]), 1, 0),) + here[: rows - 1]
+        above = here[1:rows] + (pltpu.roll(jnp.where(row == 0, side, here[0]), 7, 0),)
+        below += (pltpu.roll(jnp.where(row == 7, here[rows - 1], side), 1, 0),)
+        above += (pltpu.roll(jnp.where(row == 0, here[0], side), 7, 0),)
         return below, above
 
-    def sweep(old, new, start):
-        before, here = load(old, start - 1), load(old, start)
-        for j in range(STEP):
+    def sweep(k, start, count, reads=None):
+        old, new = ((None, v1), (v1, v2), (v2, v3))[k]
+        read = functools.partial(given, 0) if k == 0 else functools.partial(load, old)
+        reads = start if k == 0 or reads is None else reads
+        before, here = read(reads - 1), read(reads)
+        for j in range(count):
             x = start + j
-            after = load(old, x + 1)
+            after = read(reads + j + 1)
+            term = given(k + 1, x)
             below, above = along_y(here)
             for t in range(rows + 1):
-                down, up = along_z(here[t])
-                around = (before[t] + after[t]) + (below[t] + above[t]) + (down + up)
-                value = q1[x, t] + (3.0 * here[t] + around) * (1.0 / 9.0)
+                around = (before[t] + after[t]) + (below[t] + above[t]) + 3.0 * here[t]
+                value = term[t] + around * (1.0 / 9.0)
                 value = value * keep if t == rows else value
-                new[x, t] = value
+                new[BASE + x, t] = value
             before, here = here, after
-        return value
 
     def clear(field, start):
         for i in range(HALO):
-            field[start + i] = jnp.zeros((rows + 1, 8, lanes), F32)
-
-    fields = ((q1, q2), (q2, q3), (q3, q4))
-    unpack(0)
-    for k, (old, new) in enumerate(fields):
-        ends = sweep(old, new, BASE - 5 - k)
-        pl.when(first)(functools.partial(clear, new, BASE - HALO))
-
-    def advance(i, ends):
-        pl.when(i < steps - 1)(lambda: unpack(i + 1))
-        for k, (old, new) in enumerate(fields):
-            next_ends = sweep(old, new, BASE + 3 - k + i * STEP)
-            pl.when(last & (i == steps - 1))(functools.partial(clear, new, BASE + planes))
-        x0 = BASE + i * STEP
-        before, here = load(q4, x0 - 1), load(q4, x0)[:rows] + (ends,)
+            field[BASE + start + i] = jnp.zeros((rows + 1, 8, lanes), F32)
+
+    def begin(i):
+        for k, field in enumerate((v1, v2, v3)):
+            sweep(k, i * STEP - 3 + k, 6 - 2 * k)
+            if not inner and i == 0:
+                pl.when(first)(functools.partial(clear, field, -HALO))
+
+    def advance(i, at=None):
+        at = i * STEP if at is None else at
+        for k, field in enumerate((v1, v2, v3)):
+            sweep(k, i * STEP + 3 - k, STEP, at + 3 - k)
+            if not inner and i == steps - 1:
+                pl.when(last)(functools.partial(clear, field, planes))
+        x0 = i * STEP
+        before, here = load(v3, at - 1), load(v3, at)
         for j in range(STEP):
-            x = i * STEP + j
-            after = load(q4, x0 + j + 1)
+            x = x0 + j
+            after = load(v3, at + j + 1)
             below, above = along_y(here)
             for t in range(rows):
                 down, up = along_z(here[t])
@@ -256,37 +356,53 @@
             before, here = here, after
         for copy in send(i):
             copy.start()
-        return next_ends
-
-    lax.fori_loop(0, steps, advance, ends)
-
-    @pl.loop(0, steps)
-    def _(i):
-        for copy in send(i):
-            copy.wait()
-
-
-def sweeps(place, source, y_low, y_high, x_low, x_high, slabs, pencils):
-    planes, height, lanes = source.shape
-    field = pltpu.VMEM((BASE + planes + 2 * HALO, height // 8 + 1, 8, lanes), F32)
-    vmem = pl.BlockSpec(memory_space=pltpu.VMEM)
+        return at + STEP
+
+    if inner:
+        begin(1)
+        lax.fori_loop(1, steps - 1, advance, jnp.maximum(slab[0] - slabs, STEP))
+
+        @pl.loop(1, steps - 1)
+        def _(i):
+            for copy in send(i):
+                copy.wait()
+    else:
+        for i in (0, steps - 1):
+            begin(i)
+            advance(i)
+        for i in (0, steps - 1):
+            for copy in send(i):
+                copy.wait()
+
+
+def sweeps(inner, place, fields, y_faces, x_faces, results, slabs, pencils):
+    planes, rows, _, lanes = fields[0].shape
+    height = rows * 8
+    ends = pltpu.VMEM((4, BASE + planes + BASE, 8, lanes), F32)
+    field = pltpu.VMEM((BASE + planes + BASE, rows + 1, 8, lanes), F32)
+    vmem, hbm = pl.BlockSpec(memory_space=pltpu.VMEM), pl.BlockSpec(memory_space=pl.ANY)
+    scratch = [
+        ends, field, field, field,
+        pltpu.VMEM((planes, height, lanes), F32),
+        pltpu.VMEM((3, planes, height, lanes), F32),
+        pltpu.SemaphoreType.DMA((4,)),
+    ]
+    if not inner:
+        scratch.append(pltpu.VMEM((4, 2 * HALO, rows, 8, lanes), F32))
     return pl.pallas_call(
-        functools.partial(sweep_kernel, slabs, pencils),
+        functools.partial(sweep_kernel, inner, slabs, pencils),
         out_shape=[
-            jax.ShapeDtypeStruct(source.shape, F32),
-            jax.ShapeDtypeStruct((3,) + source.shape, F32),
+            jax.ShapeDtypeStruct((planes, height, lanes), F32),
+            jax.ShapeDtypeStruct((3, planes, height, lanes), F32),
         ],
-        in_specs=[pl.BlockSpec(memory_space=pltpu.SMEM)] + [vmem] * 5,
-        out_specs=[pl.BlockSpec(memory_space=pl.ANY)] * 2,
-        scratch_shapes=[
-            field, field, field, field,
-            pltpu.VMEM(source.shape, F32),
-            pltpu.VMEM((3,) + source.shape, F32),
-            pltpu.SemaphoreType.DMA((4,)),
-        ],
-        compiler_params=pltpu.CompilerParams(vmem_limit_bytes=44 << 20),
-        name="sweeps",
-    )(place, source, y_low, y_high, x_low, x_high)
+        in_specs=[pl.BlockSpec(memory_space=pltpu.SMEM)] * 2 + [vmem] * (6 + len(x_faces)) + [hbm] * len(results),
+        out_specs=[hbm, hbm],
+        scratch_shapes=scratch,
+        input_output_aliases={} if inner else {10: 0, 11: 1},
+        compiler_params=pltpu.CompilerParams(vmem_limit_bytes=28 << 20),
+        cost_estimate=pl.CostEstimate(flops=1 << 25, bytes_accessed=(24 if inner else 4) << 20, transcendentals=0),
+        name="inner_sweeps" if inner else "edge_sweeps",
+    )(*place, *fields, *y_faces, *x_faces, *results)
 
 
 def ring(values, axis, count):
@@ -298,23 +414,17 @@
 
 def on_device(fine, coarse, anchor, extent, owner, count):
     slabs, pencils = lax.axis_size("slab"), lax.axis_size("pencil")
-    sent = average(fine, anchor, extent, owner, count, slabs)
+    place = [lax.axis_index(name).astype(jnp.int32).reshape(1) for name in ("slab", "pencil")]
+    sent = average(place, fine, anchor, extent, owner, count, slabs)
     received = lax.all_to_all(sent, "slab", split_axis=0, concat_axis=0, tiled=True)
     source, y_low, y_high = deposit(received, coarse)
-    planes, height, lanes = source.shape
+    fields = prepare(source)
     y_low, y_high = ring((y_low, y_high), "pencil", pencils)
 
-    def face(at):
-        near = slice(at // 2, at // 2 + HALO // 2)
-        return jnp.concatenate(
-            [y_low[near].reshape(HALO, HALO, lanes), source[at : at + HALO],
-             y_high[near].reshape(HALO, HALO, lanes)],
-            axis=1,
-        )
-
-    x_low, x_high = ring((face(0), face(planes - HALO)), "slab", slabs)
-    place = jnp.stack([lax.axis_index("slab"), lax.axis_index("pencil")]).astype(jnp.int32)
-    potential, gradient = sweeps(place, source, y_low, y_high, x_low, x_high, slabs, pencils)
+    x_low, x_high = ring(faces(fields[0], y_low, y_high), "slab", slabs)
+    y_faces = (y_low, y_high)
+    results = sweeps(True, place, fields, y_faces, (), (), slabs, pencils)
+    potential, gradient = sweeps(False, place, fields, y_faces, (x_low, x_high), results, slabs, pencils)
     return potential, gradient
 
 

time: 85.9 us -> 77.2 us (0.90)
  the two profiles are of different devices: /device:TPU:1 before, /device:TPU:0 now
where the time goes in v2:
time: 77.2 us; the launch traced here: 76.6 us
  blocking collectives  37.5 us (49%)
  Pallas kernels  29.3 us (38%)
  starting transfers between devices  8.37 us (11%)
  between operations  1.37 us (2%)
    all_to_all x1, blocking collectives, on_device(): lax.all_to_all(sent, 'slab', split_axis=0, concat_axis=0, tiled=True)  37.5 us
    pallas_call x2, Pallas kernels, sweeps(): pl.pallas_call(functools.partial(sweep_kernel, inner, slabs, pencils), ou...  10 us
    ppermute x4, starting transfers between devices, ring(): return (lax.ppermute(high, axis, up), lax.ppermute(low, axis, down))  8.37 us
    pallas_call x1, Pallas kernels, average(): pl.pallas_call(average_kernel, out_shape=jax.ShapeDtypeStruct((slabs, row...  7.96 us
    pallas_call x1, Pallas kernels, prepare(): pl.pallas_call(prepare_kernel, out_shape=[field] * 4, in_specs=[vmem], ou...  6.63 us
    pallas_call x1, Pallas kernels, deposit(): pl.pallas_call(deposit_kernel, out_shape=[jax.ShapeDtypeStruct(coarse.sha...  4.67 us
  transfers between devices with their start and end apart: 4, of which 0 were waited for; matrix products, arithmetic and copies ran while one was open for 0% of the time, Pallas kernels for 18%

profile of v2, /device:TPU:0, one launch (start us, length us, event | category | flops | bytes accessed | tf_op | source)
XLA Modules:
  0.0 76.6 jit_solution(15849387954741579775)
XLA Ops:
  1.3 8.0 %average.1 = f32[16,264,128]{2,1,0:T(8,128)} custom-call(s32[1]{0:T(128)} %bitcast.slab, s32[1]{0:T(128)} %bitcast.1.pencil, s32[1,3,1,8]{3,2,1,0:T(1,128)} %bitcast.5, s32[1,3,1,8]{3,2,1,0:T(1,128)} %bitcast.6, s32[1,1,1,8]{3,2,1,0:T(1,128)} %bitcast.7, s32[1,1]{1,0:T(1,128)S(6)} %copy.12.count, f32[1,1,8,64,64,64]{5,4,3,2,1,0:T(8,128)} %fine.1), custom_call_target="tpu_custom_call" | custom-call | tf_op jit(solution)/shard_map/average/pallas_call | solution.py:84
  9.3 0.0 copy-start
  9.3 37.5 %all_to_all.5.received = f32[16,264,128]{2,1,0:T(8,128)S(1)} all-to-all(f32[16,264,128]{2,1,0:T(8,128)} %average.1), channel_id=1, replica_groups=mesh['slab'=16,'pencil'=8] {'slab'}, dimensions={0} | all-to-all | bytes 4325376 | tf_op jit(solution)/shard_map/all_to_all | solution.py:419
  46.8 0.0 copy-done
  46.8 4.7 %deposit.1 = (f32[96,64,128]{2,1,0:T(8,128)S(1)}, f32[48,8,128]{2,1,0:T(8,128)S(1)}, f32[48,8,128]{2,1,0:T(8,128)S(1)}) custom-call(f32[16,264,128]{2,1,0:T(8,128)S(1)} %all_to_all.5.received, f32[96,64,128]{2,1,0:T(8,128)S(1)} %copy-done), custom_call_target="tpu_custom_call" | custom-call | tf_op jit(solution)/shard_map/deposit/pallas_call | solution.py:147
  51.5 0.0 collective-permute-start
  51.5 2.9 %collective-permute-start.1 = (f32[48,8,128]{2,1,0:T(8,128)S(1)}, f32[48,8,128]{2,1,0:T(8,128)S(1)}, u32[]{:S(2)}, u32[]{:S(2)}) collective-permute-start(f32[48,8,128]{2,1,0:T(8,128)S(1)} %get-tuple-element.19), channel_id=1, source_target_pairs={{1,0},{2,1},{3,2},{4,3},{5,4},{6,5},{7,6},{0,7},{9,8},{10,9},{11,1... | collective-permute-start | bytes 589832 | tf_op jit(solution)/shard_map/ppermute | solution.py:412
  54.4 6.6 %prepare.1 = (f32[96,8,8,128]{3,2,1,0:T(8,128)S(1)}, f32[96,8,8,128]{3,2,1,0:T(8,128)S(1)}, f32[96,8,8,128]{3,2,1,0:T(8,128)S(1)}, f32[96,8,8,128]{3,2,1,0:T(8,128)S(1)}) custom-call(f32[96,64,128]{2,1,0:T(8,128)S(1)} %get-tuple-element.13.source), custom_call_target="tpu_custom_call" | custom-call | flops 33554432 | bytes 15728640 | tf_op jit(solution)/shard_map/prepare/pallas_call | solution.py:202
  61.1 0.0 collective-permute-done.y_low
  61.1 0.0 collective-permute-done.1.y_high
  61.1 0.9 %collective-permute-start.2 = (f32[4,9,8,128]{3,2,1,0:T(8,128)S(1)}, f32[4,9,8,128]{3,2,1,0:T(8,128)S(1)}, u32[]{:S(2)}, u32[]{:S(2)}) collective-permute-start(f32[4,9,8,128]{3,2,1,0:T(8,128)S(1)} %get-tuple-element.20), channel_id=1, source_target_pairs={{0,8},{8,16},{16,24},{24,32},{32,40},{40,48},{48,56},{56,64},{64,7... | collective-permute-start | bytes 442376 | tf_op jit(solution)/shard_map/ppermute | solution.py:412
  62.0 4.5 %collective-permute-start.3 = (f32[4,9,8,128]{3,2,1,0:T(8,128)S(1)}, f32[4,9,8,128]{3,2,1,0:T(8,128)S(1)}, u32[]{:S(2)}, u32[]{:S(2)}) collective-permute-start(f32[4,9,8,128]{3,2,1,0:T(8,128)S(1)} %get-tuple-element.21), channel_id=1, source_target_pairs={{8,0},{16,8},{24,16},{32,24},{40,32},{48,40},{56,48},{64,56},{72,6... | collective-permute-start | bytes 442376 | tf_op jit(solution)/shard_map/ppermute | solution.py:412
  66.5 7.3 %inner_sweeps.1 = (f32[96,64,128]{2,1,0:T(8,128)}, f32[3,96,64,128]{3,2,1,0:T(8,128)}) custom-call(s32[1]{0:T(128)} %bitcast.slab, s32[1]{0:T(128)} %bitcast.1.pencil, f32[96,8,8,128]{3,2,1,0:T(8,128)S(1)} %get-tuple-element.14.field.f0, f32[96,8,8,128]{3,2,1,0:T(8,128)S(1)} %get-tuple-element.15.f1, f32[96,8,8,128]{3,2,1,0:T(8,128)S(1)} %get-tuple-element.16.f2, ...), custom_call_target="tpu_custom_call" | custom-call | flops 33554432 | bytes 25165824 | tf_op jit(solution)/shard_map/inner_sweeps/pallas_call | solution.py:392
  73.8 0.0 collective-permute-done.2.rest_0_
  73.8 0.0 collective-permute-done.3.rest_1_
  73.8 2.7 %edge_sweeps.1 = (f32[96,64,128]{2,1,0:T(8,128)}, f32[3,96,64,128]{3,2,1,0:T(8,128)}) custom-call(s32[1]{0:T(128)} %bitcast.slab, s32[1]{0:T(128)} %bitcast.1.pencil, f32[96,8,8,128]{3,2,1,0:T(8,128)S(1)} %get-tuple-element.14.field.f0, f32[96,8,8,128]{3,2,1,0:T(8,128)S(1)} %get-tuple-element.15.f1, ...), custom_call_target="tpu_custom_call", output_to_operand_aliasing={{0}: (10, {}), {1}: (11, {})} | custom-call | flops 33554432 | bytes 4194304 | tf_op jit(solution)/shard_map/edge_sweeps/pallas_call | solution.py:392
  (1 shorter events, 0.0 us)
Async XLA Ops:
  9.3 37.5 %copy-start = (f32[96,64,128]{2,1,0:T(8,128)S(1)}, f32[96,64,128]{2,1,0:T(8,128)}, u32[]{:S(2)}) copy-start(f32[96,64,128]{2,1,0:T(8,128)} %coarse.1) | copy-start | bytes 9437188
  51.5 9.6 %collective-permute-start = (f32[48,8,128]{2,1,0:T(8,128)S(1)}, f32[48,8,128]{2,1,0:T(8,128)S(1)}, u32[]{:S(2)}, u32[]{:S(2)}) collective-permute-start(f32[48,8,128]{2,1,0:T(8,128)S(1)} %get-tuple-element.18), channel_id=1, source_target_pairs={{0,1},{1,2},{2,3},{3,4},{4,5},{5,6},{6,7},{7,0},{8,9},{9,10},{10,1... | collective-permute-start | bytes 589832 | tf_op jit(solution)/shard_map/ppermute | solution.py:412
  51.5 9.6 %collective-permute-start.1 = (f32[48,8,128]{2,1,0:T(8,128)S(1)}, f32[48,8,128]{2,1,0:T(8,128)S(1)}, u32[]{:S(2)}, u32[]{:S(2)}) collective-permute-start(f32[48,8,128]{2,1,0:T(8,128)S(1)} %get-tuple-element.19), channel_id=1, source_target_pairs={{1,0},{2,1},{3,2},{4,3},{5,4},{6,5},{7,6},{0,7},{9,8},{10,9},{11,1... | collective-permute-start | bytes 589832 | tf_op jit(solution)/shard_map/ppermute | solution.py:412
  61.1 12.7 %collective-permute-start.2 = (f32[4,9,8,128]{3,2,1,0:T(8,128)S(1)}, f32[4,9,8,128]{3,2,1,0:T(8,128)S(1)}, u32[]{:S(2)}, u32[]{:S(2)}) collective-permute-start(f32[4,9,8,128]{3,2,1,0:T(8,128)S(1)} %get-tuple-element.20), channel_id=1, source_target_pairs={{0,8},{8,16},{16,24},{24,32},{32,40},{40,48},{48,56},{56,64},{64,7... | collective-permute-start | bytes 442376 | tf_op jit(solution)/shard_map/ppermute | solution.py:412
  62.0 11.8 %collective-permute-start.3 = (f32[4,9,8,128]{3,2,1,0:T(8,128)S(1)}, f32[4,9,8,128]{3,2,1,0:T(8,128)S(1)}, u32[]{:S(2)}, u32[]{:S(2)}) collective-permute-start(f32[4,9,8,128]{3,2,1,0:T(8,128)S(1)} %get-tuple-element.21), channel_id=1, source_target_pairs={{8,0},{16,8},{24,16},{32,24},{40,32},{48,40},{56,48},{64,56},{72,6... | collective-permute-start | bytes 442376 | tf_op jit(solution)/shard_map/ppermute | solution.py:412

commit v3 on v2

--- a/solution.py
+++ b/solution.py
@@ -11,7 +11,8 @@
 META_ROWS = 8
 STEP = 8
 BASE = 8
-GROUP = 4
+GROUP = 16
+DEEP = 4
 F32 = jnp.float32
 
 
@@ -123,21 +124,33 @@
             covered = (row < hy) & (lane >= az) & (lane < az + hz)
             here = pl.ds(ay, edge)
 
-            @pl.loop(0, lax.shift_right_logical(hx + groups - 1, 2))
-            def _(tile):
-                data = received[s, pl.ds(pl.multiple_of(tile * edge, edge), edge), :]
-                for g in range(groups):
-                    i = tile * groups + g
-                    x = ax + i
-                    moved = pltpu.roll(data, lax.rem(az + lanes - g * edge, lanes), 1)
-                    change = jnp.where(covered & (i < hx), moved - coarse[x, here, :], 0.0)
-                    source[x, here, :] = source[x, here, :] + change
-
-    @pl.loop(0, planes // 2)
-    def _(k):
-        for half in range(2):
-            y_low[k, half * HALO : half * HALO + HALO, :] = source[2 * k + half, 0:HALO, :]
-            y_high[k, half * HALO : half * HALO + HALO, :] = source[2 * k + half, height - HALO : height, :]
+            @pl.loop(0, lax.div(hx + DEEP * groups - 1, DEEP * groups))
+            def _(part):
+                results = []
+                for n in range(DEEP):
+                    tile = part * DEEP + n
+                    data = received[s, pl.ds(pl.multiple_of(tile * edge, edge), edge), :]
+                    for g in range(groups):
+                        i = tile * groups + g
+                        x = ax + i
+                        moved = pltpu.roll(data, lax.rem(az + lanes - g * edge, lanes), 1)
+                        change = jnp.where(covered & (i < hx), moved - coarse[x, here, :], 0.0)
+                        results.append((x, source[x, here, :] + change))
+                for x, value in results:
+                    source[x, here, :] = value
+
+    row8 = lax.broadcasted_iota(jnp.int32, (2 * HALO, lanes), 0)
+
+    @pl.loop(0, planes // 16)
+    def _(part):
+        for j in range(8):
+            k = part * 8 + j
+            for face, start, split in ((y_low, 0, HALO), (y_high, height - 2 * HALO, 0)):
+                one, two = source[2 * k, start : start + 8, :], source[2 * k + 1, start : start + 8, :]
+                if split:
+                    face[k] = jnp.where(row8 < HALO, one, pltpu.roll(two, HALO, 0))
+                else:
+                    face[k] = jnp.where(row8 < HALO, pltpu.roll(one, HALO, 0), two)
 
 
 def deposit(received, coarse):
@@ -150,7 +163,7 @@
         in_specs=[vmem, vmem],
         out_specs=[vmem, vmem, vmem],
         scratch_shapes=[pltpu.SMEM((received.shape[0], lanes), F32), pltpu.SemaphoreType.DMA],
-        compiler_params=pltpu.CompilerParams(vmem_limit_bytes=4 << 20),
+        compiler_params=pltpu.CompilerParams(vmem_limit_bytes=12 << 20),
         name="deposit",
     )(received, coarse)
 
@@ -204,7 +217,7 @@
         out_shape=[field] * 4,
         in_specs=[vmem],
         out_specs=[vmem] * 4,
-        compiler_params=pltpu.CompilerParams(vmem_limit_bytes=4 << 20),
+        compiler_params=pltpu.CompilerParams(vmem_limit_bytes=20 << 20),
         cost_estimate=pl.CostEstimate(flops=1 << 25, bytes_accessed=15 << 20, transcendentals=0),
         name="prepare",
     )(source)

time: 77.2 us -> 73.1 us (0.947)
  Pallas kernels: 29.3 us -> 25.3 us
    pallas_call x1, Pallas kernels: 4.67 us -> 2.04 us  [deposit(): pl.pallas_call(deposit_kernel, out_shape=[jax.ShapeDtypeStruct(coarse.sha...]
    pallas_call x1, Pallas kernels: 6.63 us -> 5.29 us  [prepare(): pl.pallas_call(prepare_kernel, out_shape=[field] * 4, in_specs=[vmem], ou...]
  transfers between devices with their start and end apart: 4 -> 4, of which waited for: 0 -> 0; matrix products, arithmetic and copies ran while one was open for 0% -> 0% of each run, Pallas kernels for 18% -> 17%
where the time goes in v3:
time: 73.1 us; the launch traced here: 72.6 us
  blocking collectives  37.5 us (51%)
  Pallas kernels  25.3 us (35%)
  starting transfers between devices  8.37 us (11%)
  between operations  1.37 us (2%)
    all_to_all x1, blocking collectives, on_device(): lax.all_to_all(sent, 'slab', split_axis=0, concat_axis=0, tiled=True)  37.5 us
    pallas_call x2, Pallas kernels, sweeps(): pl.pallas_call(functools.partial(sweep_kernel, inner, slabs, pencils), ou...  10 us
    ppermute x4, starting transfers between devices, ring(): return (lax.ppermute(high, axis, up), lax.ppermute(low, axis, down))  8.37 us
    pallas_call x1, Pallas kernels, average(): pl.pallas_call(average_kernel, out_shape=jax.ShapeDtypeStruct((slabs, row...  7.96 us
    pallas_call x1, Pallas kernels, prepare(): pl.pallas_call(prepare_kernel, out_shape=[field] * 4, in_specs=[vmem], ou...  5.29 us
    pallas_call x1, Pallas kernels, deposit(): pl.pallas_call(deposit_kernel, out_shape=[jax.ShapeDtypeStruct(coarse.sha...  2.04 us
  transfers between devices with their start and end apart: 4, of which 0 were waited for; matrix products, arithmetic and copies ran while one was open for 0% of the time, Pallas kernels for 17%

profile of v3, /device:TPU:0, one launch (start us, length us, event | category | flops | bytes accessed | tf_op | source)
XLA Modules:
  0.0 72.6 jit_solution(13077134395115500482)
XLA Ops:
  1.3 8.0 %average.1 = f32[16,264,128]{2,1,0:T(8,128)} custom-call(s32[1]{0:T(128)} %bitcast.slab, s32[1]{0:T(128)} %bitcast.1.pencil, s32[1,3,1,8]{3,2,1,0:T(1,128)} %bitcast.5, s32[1,3,1,8]{3,2,1,0:T(1,128)} %bitcast.6, s32[1,1,1,8]{3,2,1,0:T(1,128)} %bitcast.7, s32[1,1]{1,0:T(1,128)S(6)} %copy.12.count, f32[1,1,8,64,64,64]{5,4,3,2,1,0:T(8,128)} %fine.1), custom_call_target="tpu_custom_call" | custom-call | tf_op jit(solution)/shard_map/average/pallas_call | solution.py:85
  9.3 0.0 copy-start
  9.3 37.5 %all_to_all.5.received = f32[16,264,128]{2,1,0:T(8,128)S(1)} all-to-all(f32[16,264,128]{2,1,0:T(8,128)} %average.1), channel_id=1, replica_groups=mesh['slab'=16,'pencil'=8] {'slab'}, dimensions={0} | all-to-all | bytes 4325376 | tf_op jit(solution)/shard_map/all_to_all | solution.py:432
  46.8 0.0 copy-done
  46.8 2.0 %deposit.1 = (f32[96,64,128]{2,1,0:T(8,128)S(1)}, f32[48,8,128]{2,1,0:T(8,128)S(1)}, f32[48,8,128]{2,1,0:T(8,128)S(1)}) custom-call(f32[16,264,128]{2,1,0:T(8,128)S(1)} %all_to_all.5.received, f32[96,64,128]{2,1,0:T(8,128)S(1)} %copy-done), custom_call_target="tpu_custom_call" | custom-call | tf_op jit(solution)/shard_map/deposit/pallas_call | solution.py:160
  48.8 0.0 collective-permute-start
  48.9 2.9 %collective-permute-start.1 = (f32[48,8,128]{2,1,0:T(8,128)S(1)}, f32[48,8,128]{2,1,0:T(8,128)S(1)}, u32[]{:S(2)}, u32[]{:S(2)}) collective-permute-start(f32[48,8,128]{2,1,0:T(8,128)S(1)} %get-tuple-element.19), channel_id=1, source_target_pairs={{1,0},{2,1},{3,2},{4,3},{5,4},{6,5},{7,6},{0,7},{9,8},{10,9},{11,1... | collective-permute-start | bytes 589832 | tf_op jit(solution)/shard_map/ppermute | solution.py:425
  51.8 5.3 %prepare.1 = (f32[96,8,8,128]{3,2,1,0:T(8,128)S(1)}, f32[96,8,8,128]{3,2,1,0:T(8,128)S(1)}, f32[96,8,8,128]{3,2,1,0:T(8,128)S(1)}, f32[96,8,8,128]{3,2,1,0:T(8,128)S(1)}) custom-call(f32[96,64,128]{2,1,0:T(8,128)S(1)} %get-tuple-element.13.source), custom_call_target="tpu_custom_call" | custom-call | flops 33554432 | bytes 15728640 | tf_op jit(solution)/shard_map/prepare/pallas_call | solution.py:215
  57.1 0.0 collective-permute-done.y_low
  57.1 0.0 collective-permute-done.1.y_high
  57.2 2.7 %collective-permute-start.2 = (f32[4,9,8,128]{3,2,1,0:T(8,128)S(1)}, f32[4,9,8,128]{3,2,1,0:T(8,128)S(1)}, u32[]{:S(2)}, u32[]{:S(2)}) collective-permute-start(f32[4,9,8,128]{3,2,1,0:T(8,128)S(1)} %get-tuple-element.20), channel_id=1, source_target_pairs={{0,8},{8,16},{16,24},{24,32},{32,40},{40,48},{48,56},{56,64},{64,7... | collective-permute-start | bytes 442376 | tf_op jit(solution)/shard_map/ppermute | solution.py:425
  59.8 2.7 %collective-permute-start.3 = (f32[4,9,8,128]{3,2,1,0:T(8,128)S(1)}, f32[4,9,8,128]{3,2,1,0:T(8,128)S(1)}, u32[]{:S(2)}, u32[]{:S(2)}) collective-permute-start(f32[4,9,8,128]{3,2,1,0:T(8,128)S(1)} %get-tuple-element.21), channel_id=1, source_target_pairs={{8,0},{16,8},{24,16},{32,24},{40,32},{48,40},{56,48},{64,56},{72,6... | collective-permute-start | bytes 442376 | tf_op jit(solution)/shard_map/ppermute | solution.py:425
  62.6 7.3 %inner_sweeps.1 = (f32[96,64,128]{2,1,0:T(8,128)}, f32[3,96,64,128]{3,2,1,0:T(8,128)}) custom-call(s32[1]{0:T(128)} %bitcast.slab, s32[1]{0:T(128)} %bitcast.1.pencil, f32[96,8,8,128]{3,2,1,0:T(8,128)S(1)} %get-tuple-element.14.field.f0, f32[96,8,8,128]{3,2,1,0:T(8,128)S(1)} %get-tuple-element.15.f1, f32[96,8,8,128]{3,2,1,0:T(8,128)S(1)} %get-tuple-element.16.f2, ...), custom_call_target="tpu_custom_call" | custom-call | flops 33554432 | bytes 25165824 | tf_op jit(solution)/shard_map/inner_sweeps/pallas_call | solution.py:405
  69.9 0.0 collective-permute-done.2.rest_0_
  69.9 0.0 collective-permute-done.3.rest_1_
  69.9 2.7 %edge_sweeps.1 = (f32[96,64,128]{2,1,0:T(8,128)}, f32[3,96,64,128]{3,2,1,0:T(8,128)}) custom-call(s32[1]{0:T(128)} %bitcast.slab, s32[1]{0:T(128)} %bitcast.1.pencil, f32[96,8,8,128]{3,2,1,0:T(8,128)S(1)} %get-tuple-element.14.field.f0, f32[96,8,8,128]{3,2,1,0:T(8,128)S(1)} %get-tuple-element.15.f1, ...), custom_call_target="tpu_custom_call", output_to_operand_aliasing={{0}: (10, {}), {1}: (11, {})} | custom-call | flops 33554432 | bytes 4194304 | tf_op jit(solution)/shard_map/edge_sweeps/pallas_call | solution.py:405
  (1 shorter events, 0.0 us)
Async XLA Ops:
  9.3 37.5 %copy-start = (f32[96,64,128]{2,1,0:T(8,128)S(1)}, f32[96,64,128]{2,1,0:T(8,128)}, u32[]{:S(2)}) copy-start(f32[96,64,128]{2,1,0:T(8,128)} %coarse.1) | copy-start | bytes 9437188
  48.8 8.3 %collective-permute-start = (f32[48,8,128]{2,1,0:T(8,128)S(1)}, f32[48,8,128]{2,1,0:T(8,128)S(1)}, u32[]{:S(2)}, u32[]{:S(2)}) collective-permute-start(f32[48,8,128]{2,1,0:T(8,128)S(1)} %get-tuple-element.18), channel_id=1, source_target_pairs={{0,1},{1,2},{2,3},{3,4},{4,5},{5,6},{6,7},{7,0},{8,9},{9,10},{10,1... | collective-permute-start | bytes 589832 | tf_op jit(solution)/shard_map/ppermute | solution.py:425
  48.9 8.3 %collective-permute-start.1 = (f32[48,8,128]{2,1,0:T(8,128)S(1)}, f32[48,8,128]{2,1,0:T(8,128)S(1)}, u32[]{:S(2)}, u32[]{:S(2)}) collective-permute-start(f32[48,8,128]{2,1,0:T(8,128)S(1)} %get-tuple-element.19), channel_id=1, source_target_pairs={{1,0},{2,1},{3,2},{4,3},{5,4},{6,5},{7,6},{0,7},{9,8},{10,9},{11,1... | collective-permute-start | bytes 589832 | tf_op jit(solution)/shard_map/ppermute | solution.py:425
  57.2 12.7 %collective-permute-start.2 = (f32[4,9,8,128]{3,2,1,0:T(8,128)S(1)}, f32[4,9,8,128]{3,2,1,0:T(8,128)S(1)}, u32[]{:S(2)}, u32[]{:S(2)}) collective-permute-start(f32[4,9,8,128]{3,2,1,0:T(8,128)S(1)} %get-tuple-element.20), channel_id=1, source_target_pairs={{0,8},{8,16},{16,24},{24,32},{32,40},{40,48},{48,56},{56,64},{64,7... | collective-permute-start | bytes 442376 | tf_op jit(solution)/shard_map/ppermute | solution.py:425
  59.8 10.0 %collective-permute-start.3 = (f32[4,9,8,128]{3,2,1,0:T(8,128)S(1)}, f32[4,9,8,128]{3,2,1,0:T(8,128)S(1)}, u32[]{:S(2)}, u32[]{:S(2)}) collective-permute-start(f32[4,9,8,128]{3,2,1,0:T(8,128)S(1)} %get-tuple-element.21), channel_id=1, source_target_pairs={{8,0},{16,8},{24,16},{32,24},{40,32},{48,40},{56,48},{64,56},{72,6... | collective-permute-start | bytes 442376 | tf_op jit(solution)/shard_map/ppermute | solution.py:425

commit v4 on v3

--- a/solution.py
+++ b/solution.py
@@ -16,39 +16,45 @@
 F32 = jnp.float32
 
 
-def average_kernel(slab, pencil, anchor, extent, owners, count, fine, sent, cells, packed, blank, in_sems, out_sem, blank_sem):
+def average_kernel(slab, pencil, anchor, extent, owners, count, fine, sent, cells, sems):
     slots, fine_edge = cells.shape[:2]
-    rows = packed.shape[1] - META_ROWS
+    rows = sent.shape[1] - META_ROWS
     edge = fine_edge // 2
-    lanes = packed.shape[2]
+    lanes = sent.shape[2]
     groups = lanes // edge
     tiles = edge // groups
-    parts = in_sems.shape[1]
-    share = fine_edge // parts
-
-    def load(p, part):
-        here = pl.ds(part * share, share)
-        return pltpu.make_async_copy(fine.at[0, 0, p, here], cells.at[p, here], in_sems.at[p, part])
-
-    def store(p):
-        return pltpu.make_async_copy(packed.at[p], sent.at[owners[0, 0, 0, p]], out_sem)
-
-    def clear():
-        return pltpu.make_async_copy(blank, sent.at[:, pl.ds(rows, META_ROWS), :], blank_sem)
-
-    for p in range(slots):
-        for part in range(parts):
-            load(p, part).start()
-    blank[...] = jnp.zeros_like(blank)
-    clear().start()
+    share = 2 * groups
+
+    def each_part(p, act):
+        planes, lines = extent[0, 0, 0, p], extent[0, 1, 0, p]
+
+        @pl.loop(0, jnp.minimum(lax.div(planes + share - 1, share), tiles))
+        def _(tile):
+            here = pl.ds(pl.multiple_of(tile * share, share), share)
+
+            def part(half):
+                there = pl.ds(half * edge, edge)
+                return pltpu.make_async_copy(fine.at[0, 0, p, here, there], cells.at[p, here, there], sems.at[p])
+
+            act(part(0))
+            pl.when(lines > edge)(lambda: act(part(1)))
+
+    live = jnp.minimum(count[0, 0], slots)
+
+    @pl.loop(0, live)
+    def _(p):
+        each_part(p, lambda copy: copy.start())
+
     lane = lax.broadcasted_iota(jnp.int32, (META_ROWS, lanes), 1)
     source_lane = lax.broadcasted_iota(jnp.int32, (fine_edge, lanes), 0)
     target_lane = lax.broadcasted_iota(jnp.int32, (fine_edge, lanes), 1)
-
-    @pl.loop(0, slots)
+    for slot in range(sent.shape[0]):
+        sent[slot, pl.ds(rows, META_ROWS), :] = jnp.zeros((META_ROWS, lanes), F32)
+
+    @pl.loop(0, live)
     def _(p):
-        for part in range(parts):
-            load(p, part).wait()
+        each_part(p, lambda copy: copy.wait())
+        owner = owners[0, 0, 0, p]
         total = jnp.zeros((rows, lanes), F32)
         for g in range(groups):
             pieces = [
@@ -61,19 +67,12 @@
             gather = jnp.where(target_lane == g * edge + source_lane // 2, 0.125, 0.0).astype(jnp.bfloat16)
             total = total + jnp.dot(high, gather, preferred_element_type=F32)
             total = total + jnp.dot(low, gather, preferred_element_type=F32)
-        packed[p, :rows, :] = total
-        alive = (p < count[0, 0]).astype(jnp.int32)
-        words = jnp.where(lane == 0, alive, 0)
+        sent[owner, :rows, :] = total
+        words = jnp.where(lane == 0, 1, 0)
         for d in range(3):
             words = jnp.where(lane == 1 + d, anchor[0, d, 0, p], words)
             words = jnp.where(lane == 4 + d, lax.shift_right_logical(extent[0, d, 0, p], 1), words)
-        packed[p, pl.ds(rows, META_ROWS), :] = words.astype(F32)
-        pl.when(p == 0)(lambda: clear().wait())
-        store(p).start()
-
-    @pl.loop(0, slots)
-    def _(p):
-        store(p).wait()
+        sent[owner, pl.ds(rows, META_ROWS), :] = words.astype(F32)
 
 
 def average(place, fine, anchor, extent, owner, count, slabs):
@@ -86,15 +85,8 @@
         average_kernel,
         out_shape=jax.ShapeDtypeStruct((slabs, rows + META_ROWS, 128), F32),
         in_specs=[smem] * 6 + [pl.BlockSpec(memory_space=pl.ANY)],
-        out_specs=pl.BlockSpec(memory_space=pl.ANY),
-        scratch_shapes=[
-            pltpu.VMEM(fine.shape[2:], F32),
-            pltpu.VMEM((slots, rows + META_ROWS, 128), F32),
-            pltpu.VMEM((slabs, META_ROWS, 128), F32),
-            pltpu.SemaphoreType.DMA((slots, 2)),
-            pltpu.SemaphoreType.DMA,
-            pltpu.SemaphoreType.DMA,
-        ],
+        out_specs=pl.BlockSpec(memory_space=pltpu.VMEM),
+        scratch_shapes=[pltpu.VMEM(fine.shape[2:], F32), pltpu.SemaphoreType.DMA((slots,))],
         compiler_params=pltpu.CompilerParams(vmem_limit_bytes=56 << 20),
         name="average",
     )(*place, by_component(anchor), by_component(extent), by_component(owner), count, fine)

time: 73.1 us -> 71.6 us (0.979)
  Pallas kernels: 25.3 us -> 23.1 us
  blocking collectives: 37.5 us -> 38.5 us
    pallas_call x1, Pallas kernels: 7.96 us -> 6.05 us  [average(): pl.pallas_call(average_kernel, out_shape=jax.ShapeDtypeStruct((slabs, row...]
    all_to_all x1, blocking collectives: 37.5 us -> 38.5 us  [on_device(): lax.all_to_all(sent, 'slab', split_axis=0, concat_axis=0, tiled=True)]
  transfers between devices with their start and end apart: 4 -> 4, of which waited for: 0 -> 0; matrix products, arithmetic and copies ran while one was open for 0% -> 0% of each run, Pallas kernels for 17% -> 18%
where the time goes in v4:
time: 71.6 us; the launch traced here: 71.4 us
  blocking collectives  38.5 us (54%)
  Pallas kernels  23.1 us (32%)
  starting transfers between devices  8.38 us (12%)
  between operations  1.36 us (2%)
    all_to_all x1, blocking collectives, on_device(): lax.all_to_all(sent, 'slab', split_axis=0, concat_axis=0, tiled=True)  38.5 us
    pallas_call x2, Pallas kernels, sweeps(): pl.pallas_call(functools.partial(sweep_kernel, inner, slabs, pencils), ou...  10 us
    ppermute x4, starting transfers between devices, ring(): return (lax.ppermute(high, axis, up), lax.ppermute(low, axis, down))  8.38 us
    pallas_call x1, Pallas kernels, average(): pl.pallas_call(average_kernel, out_shape=jax.ShapeDtypeStruct((slabs, row...  6.05 us
    pallas_call x1, Pallas kernels, prepare(): pl.pallas_call(prepare_kernel, out_shape=[field] * 4, in_specs=[vmem], ou...  5.29 us
    pallas_call x1, Pallas kernels, deposit(): pl.pallas_call(deposit_kernel, out_shape=[jax.ShapeDtypeStruct(coarse.sha...  1.75 us
  transfers between devices with their start and end apart: 4, of which 0 were waited for; matrix products, arithmetic and copies ran while one was open for 0% of the time, Pallas kernels for 18%

profile of v4, /device:TPU:0, one launch (start us, length us, event | category | flops | bytes accessed | tf_op | source)
XLA Modules:
  0.0 71.4 jit_solution(1480874206103112942)
XLA Ops:
  1.3 6.0 %average.1 = f32[16,264,128]{2,1,0:T(8,128)} custom-call(s32[1]{0:T(128)} %bitcast.slab, s32[1]{0:T(128)} %bitcast.1.pencil, s32[1,3,1,8]{3,2,1,0:T(1,128)} %bitcast.5, s32[1,3,1,8]{3,2,1,0:T(1,128)} %bitcast.6, s32[1,1,1,8]{3,2,1,0:T(1,128)} %bitcast.7, s32[1,1]{1,0:T(1,128)S(6)} %copy.12.count, f32[1,1,8,64,64,64]{5,4,3,2,1,0:T(8,128)} %fine.1), custom_call_target="tpu_custom_call" | custom-call | tf_op jit(solution)/shard_map/average/pallas_call | solution.py:84
  7.3 0.0 copy-start
  7.3 38.5 %all_to_all.5.received = f32[16,264,128]{2,1,0:T(8,128)S(1)} all-to-all(f32[16,264,128]{2,1,0:T(8,128)} %average.1), channel_id=1, replica_groups=mesh['slab'=16,'pencil'=8] {'slab'}, dimensions={0} | all-to-all | bytes 4325376 | tf_op jit(solution)/shard_map/all_to_all | solution.py:424
  45.8 0.0 copy-done
  45.8 1.8 %deposit.1 = (f32[96,64,128]{2,1,0:T(8,128)S(1)}, f32[48,8,128]{2,1,0:T(8,128)S(1)}, f32[48,8,128]{2,1,0:T(8,128)S(1)}) custom-call(f32[16,264,128]{2,1,0:T(8,128)S(1)} %all_to_all.5.received, f32[96,64,128]{2,1,0:T(8,128)S(1)} %copy-done), custom_call_target="tpu_custom_call" | custom-call | tf_op jit(solution)/shard_map/deposit/pallas_call | solution.py:152
  47.6 0.4 collective-permute-start
  47.9 2.6 %collective-permute-start.1 = (f32[48,8,128]{2,1,0:T(8,128)S(1)}, f32[48,8,128]{2,1,0:T(8,128)S(1)}, u32[]{:S(2)}, u32[]{:S(2)}) collective-permute-start(f32[48,8,128]{2,1,0:T(8,128)S(1)} %get-tuple-element.19), channel_id=1, source_target_pairs={{1,0},{2,1},{3,2},{4,3},{5,4},{6,5},{7,6},{0,7},{9,8},{10,9},{11,1... | collective-permute-start | bytes 589832 | tf_op jit(solution)/shard_map/ppermute | solution.py:417
  50.6 5.3 %prepare.1 = (f32[96,8,8,128]{3,2,1,0:T(8,128)S(1)}, f32[96,8,8,128]{3,2,1,0:T(8,128)S(1)}, f32[96,8,8,128]{3,2,1,0:T(8,128)S(1)}, f32[96,8,8,128]{3,2,1,0:T(8,128)S(1)}) custom-call(f32[96,64,128]{2,1,0:T(8,128)S(1)} %get-tuple-element.13.source), custom_call_target="tpu_custom_call" | custom-call | flops 33554432 | bytes 15728640 | tf_op jit(solution)/shard_map/prepare/pallas_call | solution.py:207
  55.9 0.0 collective-permute-done.y_low
  55.9 0.0 collective-permute-done.1.y_high
  55.9 3.1 %collective-permute-start.2 = (f32[4,9,8,128]{3,2,1,0:T(8,128)S(1)}, f32[4,9,8,128]{3,2,1,0:T(8,128)S(1)}, u32[]{:S(2)}, u32[]{:S(2)}) collective-permute-start(f32[4,9,8,128]{3,2,1,0:T(8,128)S(1)} %get-tuple-element.20), channel_id=1, source_target_pairs={{0,8},{8,16},{16,24},{24,32},{32,40},{40,48},{48,56},{56,64},{64,7... | collective-permute-start | bytes 442376 | tf_op jit(solution)/shard_map/ppermute | solution.py:417
  59.0 2.3 %collective-permute-start.3 = (f32[4,9,8,128]{3,2,1,0:T(8,128)S(1)}, f32[4,9,8,128]{3,2,1,0:T(8,128)S(1)}, u32[]{:S(2)}, u32[]{:S(2)}) collective-permute-start(f32[4,9,8,128]{3,2,1,0:T(8,128)S(1)} %get-tuple-element.21), channel_id=1, source_target_pairs={{8,0},{16,8},{24,16},{32,24},{40,32},{48,40},{56,48},{64,56},{72,6... | collective-permute-start | bytes 442376 | tf_op jit(solution)/shard_map/ppermute | solution.py:417
  61.3 7.3 %inner_sweeps.1 = (f32[96,64,128]{2,1,0:T(8,128)}, f32[3,96,64,128]{3,2,1,0:T(8,128)}) custom-call(s32[1]{0:T(128)} %bitcast.slab, s32[1]{0:T(128)} %bitcast.1.pencil, f32[96,8,8,128]{3,2,1,0:T(8,128)S(1)} %get-tuple-element.14.field.f0, f32[96,8,8,128]{3,2,1,0:T(8,128)S(1)} %get-tuple-element.15.f1, f32[96,8,8,128]{3,2,1,0:T(8,128)S(1)} %get-tuple-element.16.f2, ...), custom_call_target="tpu_custom_call" | custom-call | flops 33554432 | bytes 25165824 | tf_op jit(solution)/shard_map/inner_sweeps/pallas_call | solution.py:397
  68.6 0.0 collective-permute-done.2.rest_0_
  68.6 0.0 collective-permute-done.3.rest_1_
  68.6 2.7 %edge_sweeps.1 = (f32[96,64,128]{2,1,0:T(8,128)}, f32[3,96,64,128]{3,2,1,0:T(8,128)}) custom-call(s32[1]{0:T(128)} %bitcast.slab, s32[1]{0:T(128)} %bitcast.1.pencil, f32[96,8,8,128]{3,2,1,0:T(8,128)S(1)} %get-tuple-element.14.field.f0, f32[96,8,8,128]{3,2,1,0:T(8,128)S(1)} %get-tuple-element.15.f1, ...), custom_call_target="tpu_custom_call", output_to_operand_aliasing={{0}: (10, {}), {1}: (11, {})} | custom-call | flops 33554432 | bytes 4194304 | tf_op jit(solution)/shard_map/edge_sweeps/pallas_call | solution.py:397
  (1 shorter events, 0.0 us)
Async XLA Ops:
  7.3 38.5 %copy-start = (f32[96,64,128]{2,1,0:T(8,128)S(1)}, f32[96,64,128]{2,1,0:T(8,128)}, u32[]{:S(2)}) copy-start(f32[96,64,128]{2,1,0:T(8,128)} %coarse.1) | copy-start | bytes 9437188
  47.6 8.3 %collective-permute-start = (f32[48,8,128]{2,1,0:T(8,128)S(1)}, f32[48,8,128]{2,1,0:T(8,128)S(1)}, u32[]{:S(2)}, u32[]{:S(2)}) collective-permute-start(f32[48,8,128]{2,1,0:T(8,128)S(1)} %get-tuple-element.18), channel_id=1, source_target_pairs={{0,1},{1,2},{2,3},{3,4},{4,5},{5,6},{6,7},{7,0},{8,9},{9,10},{10,1... | collective-permute-start | bytes 589832 | tf_op jit(solution)/shard_map/ppermute | solution.py:417
  47.9 7.9 %collective-permute-start.1 = (f32[48,8,128]{2,1,0:T(8,128)S(1)}, f32[48,8,128]{2,1,0:T(8,128)S(1)}, u32[]{:S(2)}, u32[]{:S(2)}) collective-permute-start(f32[48,8,128]{2,1,0:T(8,128)S(1)} %get-tuple-element.19), channel_id=1, source_target_pairs={{1,0},{2,1},{3,2},{4,3},{5,4},{6,5},{7,6},{0,7},{9,8},{10,9},{11,1... | collective-permute-start | bytes 589832 | tf_op jit(solution)/shard_map/ppermute | solution.py:417
  55.9 12.7 %collective-permute-start.2 = (f32[4,9,8,128]{3,2,1,0:T(8,128)S(1)}, f32[4,9,8,128]{3,2,1,0:T(8,128)S(1)}, u32[]{:S(2)}, u32[]{:S(2)}) collective-permute-start(f32[4,9,8,128]{3,2,1,0:T(8,128)S(1)} %get-tuple-element.20), channel_id=1, source_target_pairs={{0,8},{8,16},{16,24},{24,32},{32,40},{40,48},{48,56},{56,64},{64,7... | collective-permute-start | bytes 442376 | tf_op jit(solution)/shard_map/ppermute | solution.py:417
  59.0 9.6 %collective-permute-start.3 = (f32[4,9,8,128]{3,2,1,0:T(8,128)S(1)}, f32[4,9,8,128]{3,2,1,0:T(8,128)S(1)}, u32[]{:S(2)}, u32[]{:S(2)}) collective-permute-start(f32[4,9,8,128]{3,2,1,0:T(8,128)S(1)} %get-tuple-element.21), channel_id=1, source_target_pairs={{8,0},{16,8},{24,16},{32,24},{40,32},{48,40},{56,48},{64,56},{72,6... | collective-permute-start | bytes 442376 | tf_op jit(solution)/shard_map/ppermute | solution.py:417

commit v5 on v4

--- a/solution.py
+++ b/solution.py
@@ -26,18 +26,12 @@
     share = 2 * groups
 
     def each_part(p, act):
-        planes, lines = extent[0, 0, 0, p], extent[0, 1, 0, p]
+        planes = extent[0, 0, 0, p]
 
         @pl.loop(0, jnp.minimum(lax.div(planes + share - 1, share), tiles))
         def _(tile):
             here = pl.ds(pl.multiple_of(tile * share, share), share)
-
-            def part(half):
-                there = pl.ds(half * edge, edge)
-                return pltpu.make_async_copy(fine.at[0, 0, p, here, there], cells.at[p, here, there], sems.at[p])
-
-            act(part(0))
-            pl.when(lines > edge)(lambda: act(part(1)))
+            act(pltpu.make_async_copy(fine.at[0, 0, p, here], cells.at[p, here], sems.at[p]))
 
     live = jnp.minimum(count[0, 0], slots)
 

time: 71.6 us -> 72 us (level)
  Pallas kernels: 23.1 us -> 24.8 us
    pallas_call x1, Pallas kernels: 1.75 us -> 2.89 us  [deposit(): pl.pallas_call(deposit_kernel, out_shape=[jax.ShapeDtypeStruct(coarse.sha...]
  transfers between devices with their start and end apart: 4 -> 4, of which waited for: 0 -> 0; matrix products, arithmetic and copies ran while one was open for 0% -> 0% of each run, Pallas kernels for 18% -> 17%
where the time goes in v5:
time: 72 us; the launch traced here: 72.4 us
  blocking collectives  37.9 us (53%)
  Pallas kernels  24.8 us (34%)
  starting transfers between devices  8.37 us (12%)
  between operations  1.38 us (2%)
    all_to_all x1, blocking collectives, on_device(): lax.all_to_all(sent, 'slab', split_axis=0, concat_axis=0, tiled=True)  37.9 us
    pallas_call x2, Pallas kernels, sweeps(): pl.pallas_call(functools.partial(sweep_kernel, inner, slabs, pencils), ou...  10 us
    ppermute x4, starting transfers between devices, ring(): return (lax.ppermute(high, axis, up), lax.ppermute(low, axis, down))  8.37 us
    pallas_call x1, Pallas kernels, average(): pl.pallas_call(average_kernel, out_shape=jax.ShapeDtypeStruct((slabs, row...  6.55 us
    pallas_call x1, Pallas kernels, prepare(): pl.pallas_call(prepare_kernel, out_shape=[field] * 4, in_specs=[vmem], ou...  5.29 us
    pallas_call x1, Pallas kernels, deposit(): pl.pallas_call(deposit_kernel, out_shape=[jax.ShapeDtypeStruct(coarse.sha...  2.89 us
  transfers between devices with their start and end apart: 4, of which 0 were waited for; matrix products, arithmetic and copies ran while one was open for 0% of the time, Pallas kernels for 17%

profile of v5, /device:TPU:0, one launch (start us, length us, event | category | flops | bytes accessed | tf_op | source)
XLA Modules:
  0.0 72.4 jit_solution(1845601699205201653)
XLA Ops:
  1.3 6.5 %average.1 = f32[16,264,128]{2,1,0:T(8,128)} custom-call(s32[1]{0:T(128)} %bitcast.slab, s32[1]{0:T(128)} %bitcast.1.pencil, s32[1,3,1,8]{3,2,1,0:T(1,128)} %bitcast.5, s32[1,3,1,8]{3,2,1,0:T(1,128)} %bitcast.6, s32[1,1,1,8]{3,2,1,0:T(1,128)} %bitcast.7, s32[1,1]{1,0:T(1,128)S(6)} %copy.12.count, f32[1,1,8,64,64,64]{5,4,3,2,1,0:T(8,128)} %fine.1), custom_call_target="tpu_custom_call" | custom-call | tf_op jit(solution)/shard_map/average/pallas_call | solution.py:78
  7.8 0.0 copy-start
  7.8 37.9 %all_to_all.5.received = f32[16,264,128]{2,1,0:T(8,128)S(1)} all-to-all(f32[16,264,128]{2,1,0:T(8,128)} %average.1), channel_id=1, replica_groups=mesh['slab'=16,'pencil'=8] {'slab'}, dimensions={0} | all-to-all | bytes 4325376 | tf_op jit(solution)/shard_map/all_to_all | solution.py:418
  45.7 0.0 copy-done
  45.7 2.9 %deposit.1 = (f32[96,64,128]{2,1,0:T(8,128)S(1)}, f32[48,8,128]{2,1,0:T(8,128)S(1)}, f32[48,8,128]{2,1,0:T(8,128)S(1)}) custom-call(f32[16,264,128]{2,1,0:T(8,128)S(1)} %all_to_all.5.received, f32[96,64,128]{2,1,0:T(8,128)S(1)} %copy-done), custom_call_target="tpu_custom_call" | custom-call | tf_op jit(solution)/shard_map/deposit/pallas_call | solution.py:146
  48.6 0.0 collective-permute-start
  48.7 2.9 %collective-permute-start.1 = (f32[48,8,128]{2,1,0:T(8,128)S(1)}, f32[48,8,128]{2,1,0:T(8,128)S(1)}, u32[]{:S(2)}, u32[]{:S(2)}) collective-permute-start(f32[48,8,128]{2,1,0:T(8,128)S(1)} %get-tuple-element.19), channel_id=1, source_target_pairs={{1,0},{2,1},{3,2},{4,3},{5,4},{6,5},{7,6},{0,7},{9,8},{10,9},{11,1... | collective-permute-start | bytes 589832 | tf_op jit(solution)/shard_map/ppermute | solution.py:411
  51.6 5.3 %prepare.1 = (f32[96,8,8,128]{3,2,1,0:T(8,128)S(1)}, f32[96,8,8,128]{3,2,1,0:T(8,128)S(1)}, f32[96,8,8,128]{3,2,1,0:T(8,128)S(1)}, f32[96,8,8,128]{3,2,1,0:T(8,128)S(1)}) custom-call(f32[96,64,128]{2,1,0:T(8,128)S(1)} %get-tuple-element.13.source), custom_call_target="tpu_custom_call" | custom-call | flops 33554432 | bytes 15728640 | tf_op jit(solution)/shard_map/prepare/pallas_call | solution.py:201
  56.9 0.0 collective-permute-done.y_low
  56.9 0.0 collective-permute-done.1.y_high
  57.0 0.1 collective-permute-start.2
  57.0 5.3 %collective-permute-start.3 = (f32[4,9,8,128]{3,2,1,0:T(8,128)S(1)}, f32[4,9,8,128]{3,2,1,0:T(8,128)S(1)}, u32[]{:S(2)}, u32[]{:S(2)}) collective-permute-start(f32[4,9,8,128]{3,2,1,0:T(8,128)S(1)} %get-tuple-element.21), channel_id=1, source_target_pairs={{8,0},{16,8},{24,16},{32,24},{40,32},{48,40},{56,48},{64,56},{72,6... | collective-permute-start | bytes 442376 | tf_op jit(solution)/shard_map/ppermute | solution.py:411
  62.4 7.3 %inner_sweeps.1 = (f32[96,64,128]{2,1,0:T(8,128)}, f32[3,96,64,128]{3,2,1,0:T(8,128)}) custom-call(s32[1]{0:T(128)} %bitcast.slab, s32[1]{0:T(128)} %bitcast.1.pencil, f32[96,8,8,128]{3,2,1,0:T(8,128)S(1)} %get-tuple-element.14.field.f0, f32[96,8,8,128]{3,2,1,0:T(8,128)S(1)} %get-tuple-element.15.f1, f32[96,8,8,128]{3,2,1,0:T(8,128)S(1)} %get-tuple-element.16.f2, ...), custom_call_target="tpu_custom_call" | custom-call | flops 33554432 | bytes 25165824 | tf_op jit(solution)/shard_map/inner_sweeps/pallas_call | solution.py:391
  69.6 0.0 collective-permute-done.2.rest_0_
  69.7 0.0 collective-permute-done.3.rest_1_
  69.7 2.7 %edge_sweeps.1 = (f32[96,64,128]{2,1,0:T(8,128)}, f32[3,96,64,128]{3,2,1,0:T(8,128)}) custom-call(s32[1]{0:T(128)} %bitcast.slab, s32[1]{0:T(128)} %bitcast.1.pencil, f32[96,8,8,128]{3,2,1,0:T(8,128)S(1)} %get-tuple-element.14.field.f0, f32[96,8,8,128]{3,2,1,0:T(8,128)S(1)} %get-tuple-element.15.f1, ...), custom_call_target="tpu_custom_call", output_to_operand_aliasing={{0}: (10, {}), {1}: (11, {})} | custom-call | flops 33554432 | bytes 4194304 | tf_op jit(solution)/shard_map/edge_sweeps/pallas_call | solution.py:391
  (1 shorter events, 0.0 us)
Async XLA Ops:
  7.8 37.9 %copy-start = (f32[96,64,128]{2,1,0:T(8,128)S(1)}, f32[96,64,128]{2,1,0:T(8,128)}, u32[]{:S(2)}) copy-start(f32[96,64,128]{2,1,0:T(8,128)} %coarse.1) | copy-start | bytes 9437188
  48.6 8.3 %collective-permute-start = (f32[48,8,128]{2,1,0:T(8,128)S(1)}, f32[48,8,128]{2,1,0:T(8,128)S(1)}, u32[]{:S(2)}, u32[]{:S(2)}) collective-permute-start(f32[48,8,128]{2,1,0:T(8,128)S(1)} %get-tuple-element.18), channel_id=1, source_target_pairs={{0,1},{1,2},{2,3},{3,4},{4,5},{5,6},{6,7},{7,0},{8,9},{9,10},{10,1... | collective-permute-start | bytes 589832 | tf_op jit(solution)/shard_map/ppermute | solution.py:411
  48.7 8.3 %collective-permute-start.1 = (f32[48,8,128]{2,1,0:T(8,128)S(1)}, f32[48,8,128]{2,1,0:T(8,128)S(1)}, u32[]{:S(2)}, u32[]{:S(2)}) collective-permute-start(f32[48,8,128]{2,1,0:T(8,128)S(1)} %get-tuple-element.19), channel_id=1, source_target_pairs={{1,0},{2,1},{3,2},{4,3},{5,4},{6,5},{7,6},{0,7},{9,8},{10,9},{11,1... | collective-permute-start | bytes 589832 | tf_op jit(solution)/shard_map/ppermute | solution.py:411
  57.0 12.7 %collective-permute-start.2 = (f32[4,9,8,128]{3,2,1,0:T(8,128)S(1)}, f32[4,9,8,128]{3,2,1,0:T(8,128)S(1)}, u32[]{:S(2)}, u32[]{:S(2)}) collective-permute-start(f32[4,9,8,128]{3,2,1,0:T(8,128)S(1)} %get-tuple-element.20), channel_id=1, source_target_pairs={{0,8},{8,16},{16,24},{24,32},{32,40},{40,48},{48,56},{56,64},{64,7... | collective-permute-start | bytes 442376 | tf_op jit(solution)/shard_map/ppermute | solution.py:411
  57.0 12.6 %collective-permute-start.3 = (f32[4,9,8,128]{3,2,1,0:T(8,128)S(1)}, f32[4,9,8,128]{3,2,1,0:T(8,128)S(1)}, u32[]{:S(2)}, u32[]{:S(2)}) collective-permute-start(f32[4,9,8,128]{3,2,1,0:T(8,128)S(1)} %get-tuple-element.21), channel_id=1, source_target_pairs={{8,0},{16,8},{24,16},{32,24},{40,32},{48,40},{56,48},{64,56},{72,6... | collective-permute-start | bytes 442376 | tf_op jit(solution)/shard_map/ppermute | solution.py:411
